TPU v7x, 32 devices: a whole 2x2x4 slice. The times are simulated.
32 devices in a mesh: dp: 8 (over y, x, core), tensor: 4 (over z).
Axes of the slice: x: 2, y: 2, z: 4, core: 2. Of those that a mesh axis runs over, the one named last changes fastest.
Arguments:
- layer_input: bfloat16 [8192, 1024], P(('dp', 'tensor')), may hold values from -6 to 6
- lengths: int32 [8], P('dp'), may hold values from 769 to 1024, as said below
- input_gain: float32 [1024], replicated, may hold values from 0.5 to 1.5
- proj_gate: bfloat16 [1024, 2048], P('dp', 'tensor'), may hold values from -0.1875 to 0.1875
- proj_values: bfloat16 [1024, 2048], P('dp', 'tensor'), may hold values from -0.1875 to 0.1875
- proj_state: bfloat16 [1024, 256], P('dp'), may hold values from -0.1875 to 0.1875
- proj_step: bfloat16 [1024, 32], P('dp', 'tensor'), may hold values from -0.1875 to 0.1875
- conv_values: float32 [4, 2048], P(None, 'tensor'), may hold values from -3 to 3
- bias_values: float32 [2048], P('tensor'), may hold values from -3 to 3
- conv_state: float32 [4, 256], replicated, may hold values from -3 to 3
- bias_state: float32 [256], replicated, may hold values from -3 to 3
- step_bias: float32 [32], P('tensor'), may hold values from -6.9 to -2.3
- decay_log: float32 [32], P('tensor'), may hold values from 0 to 2.77
- skip_gain: float32 [32], P('tensor'), may hold values from 0.5 to 1.5
- mixer_gain: float32 [2048], P('tensor'), may hold values from 0.5 to 1.5
- proj_output: bfloat16 [1024, 2048], P('dp', 'tensor'), may hold values from -0.125 to 0.125
- out_grad: bfloat16 [8192, 1024], P(('dp', 'tensor')), may hold values from -6 to 6
Outputs:
- layer_output: bfloat16 [8192, 1024], P(('dp', 'tensor'))
- input_grad: bfloat16 [8192, 1024], P(('dp', 'tensor'))
- grad_input_gain: float32 [1024], replicated
- grad_proj_gate: float32 [1024, 2048], P('dp', 'tensor')
- grad_proj_values: float32 [1024, 2048], P('dp', 'tensor')
- grad_proj_state: float32 [1024, 256], P('dp')
- grad_proj_step: float32 [1024, 32], P('dp', 'tensor')
- grad_conv_values: float32 [4, 2048], P(None, 'tensor')
- grad_bias_values: float32 [2048], P('tensor')
- grad_conv_state: float32 [4, 256], replicated
- grad_bias_state: float32 [256], replicated
- grad_step_bias: float32 [32], P('tensor')
- grad_decay_log: float32 [32], P('tensor')
- grad_skip_gain: float32 [32], P('tensor')
- grad_mixer_gain: float32 [2048], P('tensor')
- grad_proj_output: float32 [1024, 2048], P('dp', 'tensor')
Inputs may be any that keep to these rules, and one draw needn't show every extreme that they name: `lengths`: live slots of each group; its one sequence starts at the group's first slot and the rest is padding; some group is full in every draw.
All inputs are finite; a program needn't handle non-finite values.
Results may differ from a plain program's by a relative error of at most 0.015.
Values may be sent and summed in bfloat16 or wider, within the bound.
A program may use at most 128 MiB of HBM per device.

v0:
```python
from functools import partial

import jax
import jax.numpy as jnp
from jax import lax
from jax.sharding import PartitionSpec as P

CONV = 4
BLOCK = 256
INNER = 2048


HIGHEST = lax.Precision.HIGHEST
epsilon = 1e-05


def rounded(v):
    return v + lax.stop_gradient(v.astype(jnp.bfloat16).astype(jnp.float32) - v)


def causal_conv(values, kernel, conv_shift):
    length = values.shape[0]
    padded = jnp.pad(values, ((CONV - 1, 0), (0, 0)))
    summed = conv_shift + jnp.zeros_like(values)
    for offset in range(CONV):
        summed = summed + kernel[offset] * padded[offset : offset + length]
    return summed


def block_scan(carry_state, pieces, decay_rate):
    values, step_sizes, input_map, output_map = pieces
    logdecay = jnp.cumsum(step_sizes * decay_rate, axis=0)
    spread = logdecay[:, None, :] - logdecay[None, :, :]
    causal = (jnp.arange(BLOCK)[:, None] >= jnp.arange(BLOCK)[None, :])[:, :, None]
    decays = jnp.exp(jnp.where(causal, spread, -10000.0))
    scores = jnp.dot(output_map, input_map.T, precision=HIGHEST)
    weights = rounded(scores[:, :, None] * decays)
    scaled = rounded(values * step_sizes[:, :, None])
    inside = jnp.einsum("ijh,jhp->ihp", weights, scaled, precision=HIGHEST)
    carried = (
        jnp.einsum("in,hpn->ihp", output_map, carry_state, precision=HIGHEST)
        * jnp.exp(logdecay)[:, :, None]
    )
    remain = jnp.exp(logdecay[-1][None, :] - logdecay)
    new_state = carry_state * jnp.exp(logdecay[-1])[:, None, None] + jnp.einsum(
        "jhp,jn->hpn", scaled * remain[:, :, None], input_map, precision=HIGHEST
    )
    return (new_state, inside + carried)


def mixer_core(
    gate_in,
    values_in,
    state_in,
    step_in,
    conv_values,
    bias_values,
    conv_state,
    bias_state,
    step_bias,
    decay_log,
    skip_gain,
    present,
):
    length = values_in.shape[0]
    head_count = step_in.shape[1]
    head_dim = values_in.shape[1] // head_count
    state_width = state_in.shape[1] // 2
    values = rounded(jax.nn.silu(causal_conv(values_in, conv_values, bias_values)))
    state_maps = rounded(jax.nn.silu(causal_conv(state_in, conv_state, bias_state)))
    step_sizes = jax.nn.softplus(step_in + step_bias) * present[:, None]
    decay_rate = -jnp.exp(decay_log)
    blocks = length // BLOCK
    head_values = values.reshape(length, head_count, head_dim)
    pieces = (
        head_values.reshape(blocks, BLOCK, head_count, head_dim),
        step_sizes.reshape(blocks, BLOCK, head_count),
        state_maps[:, :state_width].reshape(blocks, BLOCK, state_width),
        state_maps[:, state_width:].reshape(blocks, BLOCK, state_width),
    )
    initial = jnp.zeros((head_count, head_dim, state_width), jnp.float32)
    _, outputs = lax.scan(
        jax.checkpoint(partial(block_scan, decay_rate=decay_rate)), initial, pieces
    )
    mixed = outputs.reshape(length, head_count, head_dim) + skip_gain[None, :, None] * head_values
    mixed = mixed.reshape(length, head_count * head_dim) * present[:, None]
    return mixed * jax.nn.silu(gate_in)


def contract_rows(left_side, right_side):
    return lax.dot_general(
        left_side, right_side, (((0,), (0,)), ((), ())), preferred_element_type=jnp.float32
    )


def times_transposed(left_side, right_side):
    return lax.dot_general(
        left_side, right_side, (((1,), (1,)), ((), ())), preferred_element_type=jnp.float32
    )


def project(normed, weight):
    return jnp.dot(normed, weight, preferred_element_type=jnp.float32)


def on_device(
    layer_input,
    lengths,
    input_gain,
    proj_gate,
    proj_values,
    proj_state,
    proj_step,
    conv_values,
    bias_values,
    conv_state,
    bias_state,
    step_bias,
    decay_log,
    skip_gain,
    mixer_gain,
    proj_output,
    out_grad,
):
    local_rows = layer_input.shape[0]
    rows_in = layer_input.astype(jnp.float32)
    inv_rms = lax.rsqrt(jnp.mean(rows_in * rows_in, axis=1, keepdims=True) + epsilon)
    normed_rows = (rows_in * inv_rms * input_gain).astype(jnp.bfloat16)
    normed = lax.all_gather(normed_rows, "tensor", axis=0, tiled=True)
    gate_w, values_w, state_w, step_w, output_w = (
        lax.all_gather(proj_gate, "dp", axis=0, tiled=True),
        lax.all_gather(proj_values, "dp", axis=0, tiled=True),
        lax.all_gather(proj_state, "dp", axis=0, tiled=True),
        lax.all_gather(proj_step, "dp", axis=0, tiled=True),
        lax.all_gather(proj_output, "dp", axis=0, tiled=True),
    )
    gate_in = project(normed, gate_w)
    values_in = project(normed, values_w)
    state_in = project(normed, state_w)
    step_in = project(normed, step_w)
    present = (jnp.arange(normed.shape[0]) < lengths[0]).astype(jnp.float32)
    core = partial(mixer_core, present=present)
    gated, core_pull = jax.vjp(
        core,
        gate_in,
        values_in,
        state_in,
        step_in,
        conv_values,
        bias_values,
        conv_state,
        bias_state,
        step_bias,
        decay_log,
        skip_gain,
    )
    square_sum = lax.psum(jnp.sum(gated * gated, axis=1), "tensor")
    inv_norm = lax.rsqrt(square_sum / INNER + epsilon)[:, None]
    normed_out = (gated * inv_norm * mixer_gain).astype(jnp.bfloat16)
    mixed_rows = lax.psum_scatter(
        times_transposed(normed_out, output_w), "tensor", scatter_dimension=0, tiled=True
    )
    layer_output = (rows_in + mixed_rows).astype(jnp.bfloat16)
    upstream = lax.all_gather(out_grad, "tensor", axis=0, tiled=True)
    grad_output_w = contract_rows(upstream, normed_out)
    grad_normed_out = jnp.dot(upstream, output_w, preferred_element_type=jnp.float32)
    grad_mixer_gain = jnp.sum(grad_normed_out * gated * inv_norm, axis=0)
    scaled_grad = grad_normed_out * mixer_gain
    cross = lax.psum(jnp.sum(scaled_grad * gated, axis=1), "tensor")
    grad_gated = (
        inv_norm * scaled_grad - gated * (inv_norm * inv_norm * inv_norm) * (cross / INNER)[:, None]
    )
    (
        grad_gate_in,
        grad_values_in,
        grad_state_part,
        grad_step_in,
        grad_conv_values,
        grad_bias_values,
        grad_conv_part,
        grad_shift_part,
        grad_step_bias,
        grad_decay_log,
        grad_skip_gain,
    ) = core_pull(grad_gated)
    grad_state_in, grad_conv_state, grad_bias_state = lax.psum(
        (grad_state_part, grad_conv_part, grad_shift_part), "tensor"
    )
    low_gate = grad_gate_in.astype(jnp.bfloat16)
    low_values = grad_values_in.astype(jnp.bfloat16)
    low_state = grad_state_in.astype(jnp.bfloat16)
    low_step = grad_step_in.astype(jnp.bfloat16)
    grad_gate_w = contract_rows(normed, low_gate)
    grad_values_w = contract_rows(normed, low_values)
    grad_state_w = contract_rows(normed, low_state)
    grad_step_w = contract_rows(normed, low_step)
    summed = times_transposed(low_gate, gate_w)
    summed = summed + times_transposed(low_values, values_w)
    head_part = lax.psum_scatter(
        summed + times_transposed(low_step, step_w), "tensor", scatter_dimension=0, tiled=True
    )
    own_state = lax.dynamic_slice_in_dim(
        low_state, lax.axis_index("tensor") * local_rows, local_rows, 0
    )
    grad_normed_rows = head_part + times_transposed(own_state, state_w)
    scaled_in = grad_normed_rows * input_gain
    cross_in = jnp.mean(scaled_in * rows_in, axis=1, keepdims=True)
    input_grad = (
        out_grad.astype(jnp.float32)
        + inv_rms * scaled_in
        - rows_in * (inv_rms * inv_rms * inv_rms) * cross_in
    ).astype(jnp.bfloat16)
    grad_gain_part = jnp.sum(grad_normed_rows * rows_in * inv_rms, axis=0)
    grad_gain_rows = lax.psum(grad_gain_part, "tensor")
    owned = (
        lax.psum_scatter(grad_gate_w, "dp", scatter_dimension=0, tiled=True),
        lax.psum_scatter(grad_values_w, "dp", scatter_dimension=0, tiled=True),
        lax.psum_scatter(grad_state_w, "dp", scatter_dimension=0, tiled=True),
        lax.psum_scatter(grad_step_w, "dp", scatter_dimension=0, tiled=True),
        lax.psum_scatter(grad_output_w, "dp", scatter_dimension=0, tiled=True),
    )
    totals = lax.psum(
        (
            grad_gain_rows,
            grad_conv_values,
            grad_bias_values,
            grad_conv_state,
            grad_bias_state,
            grad_step_bias,
            grad_decay_log,
            grad_skip_gain,
            grad_mixer_gain,
        ),
        "dp",
    )
    return (
        layer_output,
        input_grad,
        totals[0],
        owned[0],
        owned[1],
        owned[2],
        owned[3],
        totals[1],
        totals[2],
        totals[3],
        totals[4],
        totals[5],
        totals[6],
        totals[7],
        totals[8],
        owned[4],
    )


def solution(mesh):
    return jax.shard_map(
        on_device,
        mesh=mesh,
        in_specs=(
            P(("dp", "tensor"), None),
            P("dp"),
            P(),
            P("dp", "tensor"),
            P("dp", "tensor"),
            P("dp", None),
            P("dp", "tensor"),
            P(None, "tensor"),
            P("tensor"),
            P(),
            P(),
            P("tensor"),
            P("tensor"),
            P("tensor"),
            P("tensor"),
            P("dp", "tensor"),
            P(("dp", "tensor"), None),
        ),
        out_specs=(
            P(("dp", "tensor"), None),
            P(("dp", "tensor"), None),
            P(),
            P("dp", "tensor"),
            P("dp", "tensor"),
            P("dp", None),
            P("dp", "tensor"),
            P(None, "tensor"),
            P("tensor"),
            P(),
            P(),
            P("tensor"),
            P("tensor"),
            P("tensor"),
            P("tensor"),
            P("dp", "tensor"),
        ),
        check_vma=False,
    )
```

profile of v0, /device:TPU:9, one launch (start us, length us, event | category | flops | bytes accessed | tf_op | source)
XLA Modules:
  0.0 704.1 jit_solution(16973432411011847975)
XLA Ops:
  16.0 9.4 %all_gather.22 = bf16[1024,8]{0,1:T(8,128)(2,1)S(1)} all-gather(bf16[128,8]{0,1:T(8,128)(2,1)S(1)} %copy-done.64), channel_id=1, replica_groups=mesh['dp'=8,'tensor'=4] {'dp'}, dimensions={0}, use_global_device_ids=true | all-gather | bytes 18432 | tf_op jit(solution)/shard_map/all_gather | solution.py:134
  25.4 9.8 %all_gather.24 = bf16[1024,256]{1,0:T(8,128)(2,1)S(1)} all-gather(bf16[128,256]{1,0:T(8,128)(2,1)S(1)} %copy-done.32), channel_id=1, replica_groups=mesh['dp'=8,'tensor'=4] {'dp'}, dimensions={0}, use_global_device_ids=true | all-gather | bytes 589824 | tf_op jit(solution)/shard_map/all_gather | solution.py:133
  35.2 21.9 %all-gather.6.cloned.1.call-done = bf16[1024,1024]{1,0:T(8,128)(2,1)} async-done(((bf16[256,1024]{1,0:T(8,128)(2,1)}), bf16[1024,1024]{1,0:T(8,128)(2,1)}) %all-gather.6.cloned.1.call-update) | async-done | bytes 2097168 | tf_op jit(solution)/shard_map/all_gather | solution.py:129
  61.3 22.3 %all-gather.8.cloned.1.call-done = bf16[1024,512]{1,0:T(8,128)(2,1)} async-done(((bf16[128,512]{1,0:T(8,128)(2,1)}), bf16[1024,512]{1,0:T(8,128)(2,1)}) %all-gather.8.cloned.1.call-update) | async-done | bytes 1048592 | tf_op jit(solution)/shard_map/all_gather | solution.py:132
  86.1 2.7 subtract_add_fusion.16
  88.8 5.1 reshape.369
  93.9 3.8 copy.107
  97.7 2.9 fusion.114
  102.2 39.2 %while.41 = (s32[]{:T(128)}, f32[8,64,128]{2,1,0:T(8,128)S(1)}, f32[4,256,8,64]{1,3,2,0:T(8,128)}, f32[4,8,64,128]{3,2,1,0:T(8,128)}, f32[4,256,8]{1,2,0:T(8,128...) while((s32[]{:T(128)}, f32[8,64,128]{2,1,0:T(8,128)S(1)}, ...), condition=%wide.region_4.5_spmd.clone, body=%wide.region_1.4_spmd.clone.sunk | while | flops 911937536 | bytes 5182787 | solution.py:82
  104.5 3.7 fusion.220
  114.3 3.7 fusion.220
  124.1 3.7 fusion.220
  133.9 3.7 fusion.220
  141.4 3.8 copy.116
  145.2 4.8 reshape.366
  150.0 7.0 multiply_reduce_fusion.11
  157.0 6.9 psum.105
  163.9 4.9 convolution_bitcast_fusion.2
  169.0 11.4 %all-gather.12.cloned.1.call-done = bf16[1024,512]{1,0:T(8,128)(2,1)} async-done(((bf16[128,512]{1,0:T(8,128)(2,1)}), bf16[1024,512]{1,0:T(8,128)(2,1)}) %all-gather.12.cloned.1.call-update) | async-done | bytes 1048592 | tf_op jit(solution)/shard_map/all_gather | solution.py:135
  180.4 5.8 multiply_reduce_fusion.4
  186.2 6.8 psum.106
  193.1 6.6 multiply_reduce_fusion.5
  199.7 4.4 reshape.367
  204.1 4.2 copy.112
  212.1 104.3 %while.42 = (s32[]{:T(128)}, f32[8]{0:T(128)}, f32[8,64,128]{2,1,0:T(8,128)}, f32[4,256,8,64]{1,3,2,0:T(8,128)}, f32[4,256,8]{1,2,0:T(8,128)}, /*index=5*/f32[4,...) while((s32[]{:T(128)}, f32[8]{0:T(128)}, ...), condition=%wide.region_24.25_spmd.clone, body=%wide.region_10.24_spmd.clone.sunk | while | flops 2126804992 | bytes 16690300 | solution.py:82
  226.5 2.9 fusion.240
  230.4 2.5 reduce-window.74
  252.7 2.9 fusion.240
  278.9 2.9 fusion.240
  305.1 2.9 fusion.240
  316.4 4.0 copy.119
  320.4 4.9 reshape.368
  325.3 6.4 multiply_reduce_fusion.9
  337.3 2.7 add_add_fusion
  341.9 3.3 fusion.121
  351.0 76.4 %all-reduce.25 = bf16[1024,256]{1,0:T(8,128)(2,1)} all-reduce(f32[1024,256]{1,0:T(8,128)S(1)} %pad_add_fusion.3), channel_id=1, replica_groups=mesh['dp'=8,'tensor'=4] {'tensor'}, use_global_device_ids=true, to_apply=%region_26.27 | all-reduce | flops 262144 | bytes 1572864 | tf_op jit(solution)/shard_map/psum | solution.py:186
  427.5 2.8 fusion.139
  430.4 2.7 fusion.137
  434.3 2.6 fusion.138
  439.7 12.2 %reduce-scatter.10.cloned.1.call-done = f32[256,1024]{1,0:T(8,128)} async-done(((f32[1024,1024]{1,0:T(8,128)}), f32[256,1024]{1,0:T(8,128)}) %reduce-scatter.10.cloned.1.call-update) | async-done | bytes 1048592 | tf_op jit(solution)/shard_map/reduce_scatter | solution.py:199
  453.8 7.4 %all-reduce.23 = (f32[1024]{0:T(1024)S(1)}, f32[4,256]{1,0:T(4,128)S(1)}, f32[256]{0:T(256)S(1)}) all-reduce(f32[1024]{0:T(1024)S(1)} %get-tuple-element.742, f32[4,256]{1,0:T(4,128)S(1)} %pad_add_fusion.7, f32[256]{0:T(256)S(1)} %get-tuple-element.744), channel_id=1, replica_groups=mesh['dp'=8,'tensor'=4] {'tensor'}, use_global_device_ids=true, to_apply=%region_29.30 | all-reduce | flops 2304 | bytes 18432 | tf_op jit(solution)/shard_map/psum | solution.py:214
  461.2 22.8 %all-reduce.22 = (f32[1024]{0:T(1024)}, f32[4,512]{1,0:T(4,128)}, f32[512]{0:T(512)}, f32[4,256]{1,0:T(4,128)}, f32[256]{0:T(256)}, /*index=5*/f32[8]{0:T(128)}, f32[8]{0:T(128)}, f32[8]{0:T(128)}, f32[512]{0:T(512)}) all-reduce(f32[1024]{0:T(1024)S(1)} %get-tuple-element.802, ...), channel_id=1, replica_groups=mesh['dp'=8,'tensor'=4] {'dp'}, use_global_device_ids=true, to_apply=%region_30.31 | all-reduce | flops 5400 | bytes 43200 | tf_op jit(solution)/shard_map/psum | solution.py:222
  484.0 47.4 %reduce-scatter.8.cloned.1.call-done = f32[256,1024]{1,0:T(8,128)} async-done(((f32[1024,1024]{1,0:T(8,128)}), f32[256,1024]{1,0:T(8,128)}) %reduce-scatter.8.cloned.1.call-update) | async-done | bytes 1048592 | tf_op jit(solution)/shard_map/reduce_scatter | solution.py:160
  531.3 2.6 fusion.104
  533.9 32.5 %reduce-scatter.18.cloned.1.call-done = f32[128,8]{0,1:T(8,128)} async-done(((f32[1024,8]{0,1:T(8,128)}), f32[128,8]{0,1:T(8,128)}) %reduce-scatter.18.cloned.1.call-update) | async-done | bytes 4112 | tf_op jit(solution)/shard_map/reduce_scatter | solution.py:219
  566.5 40.0 %reduce-scatter.16.cloned.1.call-done = f32[128,256]{1,0:T(8,128)} async-done(((f32[1024,256]{1,0:T(8,128)}), f32[128,256]{1,0:T(8,128)}) %reduce-scatter.16.cloned.1.call-update) | async-done | bytes 131088 | tf_op jit(solution)/shard_map/reduce_scatter | solution.py:218
  606.5 45.2 %reduce-scatter.12.cloned.1.call-done = f32[128,512]{1,0:T(8,128)} async-done(((f32[1024,512]{1,0:T(8,128)}), f32[128,512]{1,0:T(8,128)}) %reduce-scatter.12.cloned.1.call-update) | async-done | bytes 262160 | tf_op jit(solution)/shard_map/reduce_scatter | solution.py:216
  651.7 45.3 %reduce-scatter.14.cloned.1.call-done = f32[128,512]{1,0:T(8,128)} async-done(((f32[1024,512]{1,0:T(8,128)}), f32[128,512]{1,0:T(8,128)}) %reduce-scatter.14.cloned.1.call-update) | async-done | bytes 262160 | tf_op jit(solution)/shard_map/reduce_scatter | solution.py:217
  (450 shorter events, 152.4 us)
Async XLA Ops:
  7.2 8.0 %copy-start.71 = (f32[8]{0:T(128)S(1)}, f32[8]{0:T(128)}, u32[]{:S(2)}) copy-start(f32[8]{0:T(128)} %param.33) | copy-start | bytes 100
  7.2 8.5 %copy-start.68 = (f32[8]{0:T(128)S(1)}, f32[8]{0:T(128)}, u32[]{:S(2)}) copy-start(f32[8]{0:T(128)} %param.34) | copy-start | bytes 100
  7.2 8.7 %copy-start.62 = (f32[4,256]{1,0:T(4,128)S(1)}, f32[4,256]{1,0:T(4,128)}, u32[]{:S(2)}) copy-start(f32[4,256]{1,0:T(4,128)} %param.30) | copy-start | bytes 12292
  7.2 8.7 %copy-start.59 = (f32[4,512]{1,0:T(4,128)S(1)}, f32[4,512]{1,0:T(4,128)}, u32[]{:S(2)}) copy-start(f32[4,512]{1,0:T(4,128)} %param.28) | copy-start | bytes 24580
  7.2 8.7 %copy-start.64 = (bf16[128,8]{0,1:T(8,128)(2,1)S(1)}, bf16[128,8]{0,1:T(8,128)(2,1)}, u32[]{:S(2)}) copy-start(bf16[128,8]{0,1:T(8,128)(2,1)} %param.27) | copy-start | bytes 6148
  7.2 18.2 %copy-start.32 = (bf16[128,256]{1,0:T(8,128)(2,1)S(1)}, bf16[128,256]{1,0:T(8,128)(2,1)}, u32[]{:S(2)}) copy-start(bf16[128,256]{1,0:T(8,128)(2,1)} %param.26) | copy-start | bytes 196612
  7.2 49.9 %all-gather.6.cloned.1.call-start = ((), (), s32[]{:S(2)}) async-start(), calls=%async_computation.7 | async-start | bytes 2621440 | tf_op jit(solution)/shard_map/all_gather | solution.py:129
  11.8 71.8 %all-gather.8.cloned.1.call-start = ((), (), s32[]{:S(2)}) async-start(), calls=%async_computation.8 | async-start | bytes 1179648 | tf_op jit(solution)/shard_map/all_gather | solution.py:132
  12.5 137.5 %all-gather.10.cloned.1.call-start = ((), (), s32[]{:S(2)}) async-start(), calls=%async_computation.9 | async-start | bytes 1179648 | tf_op jit(solution)/shard_map/all_gather | solution.py:131
  13.2 150.7 %all-gather.14.cloned.1.call-start = ((), (), s32[]{:S(2)}) async-start(), calls=%async_computation.12 | async-start | bytes 2621440 | tf_op jit(solution)/shard_map/all_gather | solution.py:164
  13.8 166.6 %all-gather.12.cloned.1.call-start = ((), (), s32[]{:S(2)}) async-start(), calls=%async_computation.10 | async-start | bytes 1179648 | tf_op jit(solution)/shard_map/all_gather | solution.py:135
  14.4 423.5 %reduce-scatter.20.cloned.1.call-start = ((), (), s32[]{:S(2)}) async-start(), calls=%async_computation.18 | async-start | bytes 2359296 | tf_op jit(solution)/shard_map/reduce_scatter | solution.py:220
  15.7 177.3 %copy-start.30 = (f32[1024]{0:T(1024)}, f32[1024]{0:T(1024)S(1)}, u32[]{:S(2)}) copy-start(f32[1024]{0:T(1024)S(1)} %fusion.118) | copy-start | bytes 12292
  15.9 177.2 %copy-start.44 = (f32[512]{0:T(512)}, f32[512]{0:T(512)S(1)}, u32[]{:S(2)}) copy-start(f32[512]{0:T(512)S(1)} %mul.802) | copy-start | bytes 6148
  15.9 43.6 %copy-start.51 = (f32[1,256]{1,0:T(1,128)}, f32[1,256]{1,0:T(1,128)S(1)}, u32[]{:S(2)}) copy-start(f32[1,256]{1,0:T(1,128)S(1)} %get-tuple-element.849) | copy-start | bytes 3076
  15.9 43.6 %copy-start.53 = (f32[1,256]{1,0:T(1,128)}, f32[1,256]{1,0:T(1,128)S(1)}, u32[]{:S(2)}) copy-start(f32[1,256]{1,0:T(1,128)S(1)} %get-tuple-element.850) | copy-start | bytes 3076
  15.9 43.6 %copy-start.55 = (f32[1,256]{1,0:T(1,128)}, f32[1,256]{1,0:T(1,128)S(1)}, u32[]{:S(2)}) copy-start(f32[1,256]{1,0:T(1,128)S(1)} %get-tuple-element.851) | copy-start | bytes 3076
  15.9 43.6 %copy-start.57 = (f32[1,256]{1,0:T(1,128)}, f32[1,256]{1,0:T(1,128)S(1)}, u32[]{:S(2)}) copy-start(f32[1,256]{1,0:T(1,128)S(1)} %get-tuple-element.852) | copy-start | bytes 3076
  15.9 70.1 %copy-start.34 = (f32[1,512]{1,0:T(1,128)}, f32[1,512]{1,0:T(1,128)S(1)}, u32[]{:S(2)}) copy-start(f32[1,512]{1,0:T(1,128)S(1)} %get-tuple-element.843) | copy-start | bytes 6148
  16.0 70.1 %copy-start.36 = (f32[1,512]{1,0:T(1,128)}, f32[1,512]{1,0:T(1,128)S(1)}, u32[]{:S(2)}) copy-start(f32[1,512]{1,0:T(1,128)S(1)} %get-tuple-element.844) | copy-start | bytes 6148
  16.0 70.1 %copy-start.38 = (f32[1,512]{1,0:T(1,128)}, f32[1,512]{1,0:T(1,128)S(1)}, u32[]{:S(2)}) copy-start(f32[1,512]{1,0:T(1,128)S(1)} %get-tuple-element.845) | copy-start | bytes 6148
  16.0 70.1 %copy-start.40 = (f32[1,512]{1,0:T(1,128)}, f32[1,512]{1,0:T(1,128)S(1)}, u32[]{:S(2)}) copy-start(f32[1,512]{1,0:T(1,128)S(1)} %get-tuple-element.846) | copy-start | bytes 6148
  25.4 72.3 %copy-start.26 = (bf16[1024,8]{0,1:T(8,128)(2,1)}, bf16[1024,8]{0,1:T(8,128)(2,1)S(1)}, u32[]{:S(2)}) copy-start(bf16[1024,8]{0,1:T(8,128)(2,1)S(1)} %all_gather.22) | copy-start | bytes 49156
  35.2 24.2 %copy-start.11 = (bf16[1024,256]{1,0:T(8,128)(2,1)}, bf16[1024,256]{1,0:T(8,128)(2,1)S(1)}, u32[]{:S(2)}) copy-start(bf16[1024,256]{1,0:T(8,128)(2,1)S(1)} %all_gather.24) | copy-start | bytes 1572868
  35.2 24.3 %copy-start.66 = (f32[256]{0:T(256)S(1)}, f32[256]{0:T(256)}, u32[]{:S(2)}) copy-start(f32[256]{0:T(256)} %param.31) | copy-start | bytes 3076
  59.5 24.0 %copy-start.4 = (bf16[1024,1024]{1,0:T(8,128)(2,1)S(1)}, bf16[1024,1024]{1,0:T(8,128)(2,1)}, u32[]{:S(2)}) copy-start(bf16[1024,1024]{1,0:T(8,128)(2,1)} %all-gather.6.cloned.1.call-done) | copy-start | bytes 6291460
  61.3 24.8 %copy-start.63 = (f32[512]{0:T(512)S(1)}, f32[512]{0:T(512)}, u32[]{:S(2)}) copy-start(f32[512]{0:T(512)} %param.29) | copy-start | bytes 6148
  88.8 104.2 %copy-start = (f32[1024,512]{1,0:T(8,128)}, f32[1024,512]{1,0:T(8,128)S(1)}, u32[]{:S(2)}) copy-start(f32[1024,512]{1,0:T(8,128)S(1)} %get-tuple-element.822) | copy-start | bytes 6291460
  150.0 13.9 %copy-start.42 = (f32[512]{0:T(512)S(1)}, f32[512]{0:T(512)}, u32[]{:S(2)}) copy-start(f32[512]{0:T(512)} %param.35) | copy-start | bytes 6148
  163.9 29.2 %copy-start.24 = (f32[1024]{0:T(1024)}, f32[1024]{0:T(1024)S(1)}, u32[]{:S(2)}) copy-start(f32[1024]{0:T(1024)S(1)} %get-tuple-element.848) | copy-start | bytes 12292
  168.9 283.0 %reduce-scatter.10.cloned.1.call-start = ((), (), s32[]{:S(2)}) async-start(), calls=%async_computation.13 | async-start | bytes 5242880 | tf_op jit(solution)/shard_map/reduce_scatter | solution.py:199
  218.8 10.6 %copy-start.23 = (f32[8]{0:T(128)}, f32[8]{0:T(128)S(1)}, u32[]{:S(2)}) copy-start(f32[8]{0:T(128)S(1)} %get-tuple-element.1055) | copy-start | bytes 100 | tf_op jit(solution)/shard_map/transpose(jvp())/while
  226.5 6.8 copy-start.48
  245.0 10.6 %copy-start.23 = (f32[8]{0:T(128)}, f32[8]{0:T(128)S(1)}, u32[]{:S(2)}) copy-start(f32[8]{0:T(128)S(1)} %get-tuple-element.1055) | copy-start | bytes 100 | tf_op jit(solution)/shard_map/transpose(jvp())/while
  271.2 10.6 %copy-start.23 = (f32[8]{0:T(128)}, f32[8]{0:T(128)S(1)}, u32[]{:S(2)}) copy-start(f32[8]{0:T(128)S(1)} %get-tuple-element.1055) | copy-start | bytes 100 | tf_op jit(solution)/shard_map/transpose(jvp())/while
  297.5 10.6 %copy-start.23 = (f32[8]{0:T(128)}, f32[8]{0:T(128)S(1)}, u32[]{:S(2)}) copy-start(f32[8]{0:T(128)S(1)} %get-tuple-element.1055) | copy-start | bytes 100 | tf_op jit(solution)/shard_map/transpose(jvp())/while
  340.1 191.3 %reduce-scatter.8.cloned.1.call-start = ((), (), s32[]{:S(2)}) async-start(), calls=%async_computation.11 | async-start | bytes 5242880 | tf_op jit(solution)/shard_map/reduce_scatter | solution.py:160
  345.2 221.3 %reduce-scatter.18.cloned.1.call-start = ((), (), s32[]{:S(2)}) async-start(), calls=%async_computation.17 | async-start | bytes 36864 | tf_op jit(solution)/shard_map/reduce_scatter | solution.py:219
  427.4 179.0 %reduce-scatter.16.cloned.1.call-start = ((), (), s32[]{:S(2)}) async-start(), calls=%async_computation.16 | async-start | bytes 1179648 | tf_op jit(solution)/shard_map/reduce_scatter | solution.py:218
  430.3 221.4 %reduce-scatter.12.cloned.1.call-start = ((), (), s32[]{:S(2)}) async-start(), calls=%async_computation.14 | async-start | bytes 2359296 | tf_op jit(solution)/shard_map/reduce_scatter | solution.py:216
  433.1 263.9 %reduce-scatter.14.cloned.1.call-start = ((), (), s32[]{:S(2)}) async-start(), calls=%async_computation.15 | async-start | bytes 2359296 | tf_op jit(solution)/shard_map/reduce_scatter | solution.py:217
  436.9 14.9 %copy-start.3 = (bf16[256,1024]{1,0:T(8,128)(2,1)S(1)}, bf16[256,1024]{1,0:T(8,128)(2,1)}, u32[]{:S(2)}) copy-start(bf16[256,1024]{1,0:T(8,128)(2,1)} %param.21) | copy-start | bytes 1572868
  436.9 14.9 %copy-start.12 = (bf16[1024,256]{1,0:T(8,128)(2,1)S(1)}, bf16[1024,256]{1,0:T(8,128)(2,1)}, u32[]{:S(2)}) copy-start(bf16[1024,256]{1,0:T(8,128)(2,1)} %copy-done.11) | copy-start | bytes 1572868
  437.0 14.9 %copy-start.33 = (f32[1024]{0:T(1024)S(1)}, f32[1024]{0:T(1024)}, u32[]{:S(2)}) copy-start(f32[1024]{0:T(1024)} %param.23) | copy-start | bytes 12292
  437.0 14.9 %copy-start.47 = (f32[256]{0:T(256)S(1)}, f32[256]{0:T(256)}, u32[]{:S(2)}) copy-start(f32[256]{0:T(256)} %copy-done.46) | copy-start | bytes 3076
  437.0 24.2 %copy-start.65 = (f32[512]{0:T(512)S(1)}, f32[512]{0:T(512)}, u32[]{:S(2)}) copy-start(f32[512]{0:T(512)} %get-tuple-element.731) | copy-start | bytes 6148
  437.0 94.3 %copy-start.10 = (bf16[256,1024]{1,0:T(8,128)(2,1)S(1)}, bf16[256,1024]{1,0:T(8,128)(2,1)}, u32[]{:S(2)}) copy-start(bf16[256,1024]{1,0:T(8,128)(2,1)} %param.37) | copy-start | bytes 1572868
  437.0 94.3 %copy-start.61 = (f32[256]{0:T(256)S(1)}, f32[256]{0:T(256)}, u32[]{:S(2)}) copy-start(f32[256]{0:T(256)} %get-tuple-element.853) | copy-start | bytes 3076
  (55 other events, 162.5 us)
Sparse Core Ops, SparseCore 0:
  11.9 45.2 all-gather.5
  59.0 24.4 all-gather.7
  85.5 23.4 all-gather.9
  110.4 43.6 all-gather.13
  155.9 24.4 all-gather.11
  183.5 40.7 reduce-scatter.19
  340.2 111.6 reduce-scatter.9
  454.2 77.1 reduce-scatter.7
  535.2 31.2 reduce-scatter.17
  570.1 36.3 reduce-scatter.15
  610.3 41.3 reduce-scatter.11
  655.8 41.2 reduce-scatter.13
where the time goes:
time: 712 us; the launch traced here: 704 us
  waiting for transfers between devices  281 us (39%)
  blocking collectives  140 us (20%)
  matrix products  124 us (17%)
  other arithmetic  76.4 us (11%)
  local copies, waits for them, and re-layouts  65.2 us (9%)
  between operations  15.9 us (2%)
    psum x1, blocking collectives, on_device(): lax.psum((grad_state_part, grad_conv_part, grad_shift_part), 'tensor')  76.4 us
    reduce_scatter x1, waiting for transfers between devices, on_device(): lax.psum_scatter(times_transposed(normed_out, output_w), 'tensor', scatte...  47.4 us
    reduce_scatter x1, waiting for transfers between devices, on_device(): lax.psum_scatter(grad_values_w, 'dp', scatter_dimension=0, tiled=True)  45.3 us
    reduce_scatter x1, waiting for transfers between devices, on_device(): lax.psum_scatter(grad_gate_w, 'dp', scatter_dimension=0, tiled=True)  45.2 us
    reduce_scatter x1, waiting for transfers between devices, on_device(): lax.psum_scatter(grad_state_w, 'dp', scatter_dimension=0, tiled=True)  40 us
    dot_general x12, matrix products, block_scan(): inside = jnp.einsum('ijh,jhp->ihp', weights, scaled, precision=HIGHEST)  34.6 us
    reduce_scatter x1, waiting for transfers between devices, on_device(): lax.psum_scatter(grad_step_w, 'dp', scatter_dimension=0, tiled=True)  32.5 us
    another operation x37, other arithmetic  25.1 us
  transfers between devices with their start and end apart: 12, of which 9 were waited for; matrix products, arithmetic and copies ran while one was open for 36% of the time, Pallas kernels for 0%

commit v1 on v0

--- a/solution.py
+++ b/solution.py
@@ -3,6 +3,8 @@
 import jax
 import jax.numpy as jnp
 from jax import lax
+from jax.experimental import pallas as pl
+from jax.experimental.pallas import tpu as pltpu
 from jax.sharding import PartitionSpec as P
 
 CONV = 4
@@ -87,6 +89,135 @@
     return mixed * jax.nn.silu(gate_in)
 
 
+def exchange_kernel(plan, sizes, *refs):
+    count = len(plan)
+    ins, outs = refs[:count], refs[count : 2 * count]
+    slots = refs[2 * count : 3 * count]
+    send_sem, recv_sem = refs[3 * count :]
+    axes = sorted({axis for _, axis in plan})
+    me = {axis: lax.axis_index(axis) for axis in axes}
+    barrier = pltpu.get_barrier_semaphore()
+    greeted = 0
+    for axis in axes:
+        size = sizes[axis]
+        for step in range(1, size):
+            peer = lax.rem(me[axis] + step, size)
+            pl.semaphore_signal(
+                barrier, inc=1, device_id={axis: peer}, device_id_type=pl.DeviceIdType.MESH
+            )
+            greeted += 1
+    pl.semaphore_wait(barrier, greeted)
+
+    def describe(item, step):
+        kind, axis = plan[item]
+        size = sizes[axis]
+        peer = lax.rem(me[axis] + step, size)
+        if kind == "gather":
+            rows = ins[item].shape[0]
+            source = ins[item]
+            target = outs[item].at[pl.ds(pl.multiple_of(me[axis] * rows, rows), rows)]
+        elif kind == "scatter":
+            rows = outs[item].shape[0]
+            source = ins[item].at[pl.ds(pl.multiple_of(peer * rows, rows), rows)]
+            target = slots[item].at[me[axis]]
+        else:
+            source, target = ins[item], slots[item].at[me[axis]]
+        return pltpu.make_async_remote_copy(
+            src_ref=source,
+            dst_ref=target,
+            send_sem=send_sem.at[item, step],
+            recv_sem=recv_sem.at[item, step],
+            device_id={axis: peer},
+            device_id_type=pl.DeviceIdType.MESH,
+        )
+
+    def arrival(item, step):
+        kind, axis = plan[item]
+        size = sizes[axis]
+        origin = lax.rem(me[axis] + size - step, size)
+        if kind == "gather":
+            rows = ins[item].shape[0]
+            target = outs[item].at[pl.ds(pl.multiple_of(origin * rows, rows), rows)]
+        else:
+            target = slots[item].at[origin]
+        return pltpu.make_async_remote_copy(
+            src_ref=target,
+            dst_ref=target,
+            send_sem=send_sem.at[item, step],
+            recv_sem=recv_sem.at[item, step],
+            device_id={axis: origin},
+            device_id_type=pl.DeviceIdType.MESH,
+        )
+
+    most = max(sizes[axis] for axis in axes)
+    sent = []
+    for step in range(1, most):
+        for item in range(count):
+            if step < sizes[plan[item][1]]:
+                copy = describe(item, step)
+                copy.start()
+                sent.append(copy)
+    for item in range(count):
+        kind, axis = plan[item]
+        if kind == "gather":
+            rows = ins[item].shape[0]
+            outs[item][pl.ds(pl.multiple_of(me[axis] * rows, rows), rows), :] = ins[item][...]
+        elif kind == "sum":
+            slots[item][me[axis]] = ins[item][...]
+    for item in range(count):
+        kind, axis = plan[item]
+        size = sizes[axis]
+        for step in range(1, size):
+            arrival(item, step).wait_recv()
+        if kind == "scatter":
+            rows = outs[item].shape[0]
+            total = ins[item][pl.ds(pl.multiple_of(me[axis] * rows, rows), rows), :].astype(jnp.float32)
+            for step in range(1, size):
+                origin = lax.rem(me[axis] + size - step, size)
+                total = total + slots[item][origin].astype(jnp.float32)
+            outs[item][...] = total
+        elif kind == "sum":
+            total = slots[item][0].astype(jnp.float32)
+            for index in range(1, size):
+                total = total + slots[item][index].astype(jnp.float32)
+            outs[item][...] = total
+    for copy in sent:
+        copy.wait_send()
+
+
+def exchange(identity, *items):
+    sizes = {axis: lax.axis_size(axis) for _, axis, _ in items}
+    plan, shapes, slots = [], [], []
+    for kind, axis, array in items:
+        size = sizes[axis]
+        rows, columns = array.shape
+        plan.append((kind, axis))
+        if kind == "gather":
+            shapes.append(jax.ShapeDtypeStruct((size * rows, columns), array.dtype))
+            slots.append(pltpu.VMEM((1, 16, 128), array.dtype))
+        elif kind == "scatter":
+            shapes.append(jax.ShapeDtypeStruct((rows // size, columns), jnp.float32))
+            slots.append(pltpu.VMEM((size, rows // size, columns), array.dtype))
+        else:
+            shapes.append(jax.ShapeDtypeStruct((rows, columns), jnp.float32))
+            slots.append(pltpu.VMEM((size, rows, columns), array.dtype))
+    most = max(sizes.values())
+    return pl.pallas_call(
+        partial(exchange_kernel, tuple(plan), sizes),
+        out_shape=tuple(shapes),
+        in_specs=[pl.BlockSpec(memory_space=pltpu.VMEM)] * len(items),
+        out_specs=tuple([pl.BlockSpec(memory_space=pltpu.VMEM)] * len(items)),
+        scratch_shapes=slots
+        + [
+            pltpu.SemaphoreType.DMA((len(items), most)),
+            pltpu.SemaphoreType.DMA((len(items), most)),
+        ],
+        compiler_params=pltpu.CompilerParams(
+            collective_id=identity, has_side_effects=True, vmem_limit_bytes=48 * 2**20
+        ),
+    )(*[array for _, _, array in items])
+
+
 def contract_rows(left_side, right_side):
     return lax.dot_general(
         left_side, right_side, (((0,), (0,)), ((), ())), preferred_element_type=jnp.float32
@@ -126,14 +257,23 @@
     rows_in = layer_input.astype(jnp.float32)
     inv_rms = lax.rsqrt(jnp.mean(rows_in * rows_in, axis=1, keepdims=True) + epsilon)
     normed_rows = (rows_in * inv_rms * input_gain).astype(jnp.bfloat16)
-    normed = lax.all_gather(normed_rows, "tensor", axis=0, tiled=True)
-    gate_w, values_w, state_w, step_w, output_w = (
-        lax.all_gather(proj_gate, "dp", axis=0, tiled=True),
-        lax.all_gather(proj_values, "dp", axis=0, tiled=True),
-        lax.all_gather(proj_state, "dp", axis=0, tiled=True),
-        lax.all_gather(proj_step, "dp", axis=0, tiled=True),
-        lax.all_gather(proj_output, "dp", axis=0, tiled=True),
-    )
+    state_columns = proj_state.shape[1]
+    head_count = proj_step.shape[1]
+    tail = -(state_columns + head_count) % 128
+    small_w = jnp.concatenate(
+        [proj_state, proj_step, jnp.zeros((proj_step.shape[0], tail), jnp.bfloat16)], axis=1
+    )
+    normed, gate_w, values_w, small_w = exchange(
+        0,
+        ("gather", "tensor", normed_rows),
+        ("gather", "dp", proj_gate),
+        ("gather", "dp", proj_values),
+        ("gather", "dp", small_w),
+    )
+    state_w = small_w[:, :state_columns]
+    step_w = small_w[:, state_columns : state_columns + head_count]
+    output_w = lax.all_gather(proj_output, "dp", axis=0, tiled=True)
+    upstream = lax.all_gather(out_grad, "tensor", axis=0, tiled=True)
     gate_in = project(normed, gate_w)
     values_in = project(normed, values_w)
     state_in = project(normed, state_w)
@@ -154,19 +294,21 @@
         decay_log,
         skip_gain,
     )
-    square_sum = lax.psum(jnp.sum(gated * gated, axis=1), "tensor")
-    inv_norm = lax.rsqrt(square_sum / INNER + epsilon)[:, None]
+    grad_normed_out = jnp.dot(upstream, output_w, preferred_element_type=jnp.float32)
+    scaled_grad = grad_normed_out * mixer_gain
+    row_sums = jnp.stack([jnp.sum(gated * gated, axis=1), jnp.sum(scaled_grad * gated, axis=1)])
+    (row_sums,) = exchange(
+        1, ("sum", "tensor", jnp.pad(row_sums, ((0, 6), (0, 0))))
+    )
+    inv_norm = lax.rsqrt(row_sums[0] / INNER + epsilon)[:, None]
+    cross = row_sums[1]
     normed_out = (gated * inv_norm * mixer_gain).astype(jnp.bfloat16)
     mixed_rows = lax.psum_scatter(
         times_transposed(normed_out, output_w), "tensor", scatter_dimension=0, tiled=True
     )
     layer_output = (rows_in + mixed_rows).astype(jnp.bfloat16)
-    upstream = lax.all_gather(out_grad, "tensor", axis=0, tiled=True)
     grad_output_w = contract_rows(upstream, normed_out)
-    grad_normed_out = jnp.dot(upstream, output_w, preferred_element_type=jnp.float32)
     grad_mixer_gain = jnp.sum(grad_normed_out * gated * inv_norm, axis=0)
-    scaled_grad = grad_normed_out * mixer_gain
-    cross = lax.psum(jnp.sum(scaled_grad * gated, axis=1), "tensor")
     grad_gated = (
         inv_norm * scaled_grad - gated * (inv_norm * inv_norm * inv_norm) * (cross / INNER)[:, None]
     )
@@ -183,24 +325,31 @@
         grad_decay_log,
         grad_skip_gain,
     ) = core_pull(grad_gated)
-    grad_state_in, grad_conv_state, grad_bias_state = lax.psum(
-        (grad_state_part, grad_conv_part, grad_shift_part), "tensor"
-    )
+    (own_state,) = exchange(2, ("scatter", "tensor", grad_state_part.astype(jnp.bfloat16)))
+    own_state = own_state.astype(jnp.bfloat16)
     low_gate = grad_gate_in.astype(jnp.bfloat16)
     low_values = grad_values_in.astype(jnp.bfloat16)
-    low_state = grad_state_in.astype(jnp.bfloat16)
     low_step = grad_step_in.astype(jnp.bfloat16)
     grad_gate_w = contract_rows(normed, low_gate)
     grad_values_w = contract_rows(normed, low_values)
-    grad_state_w = contract_rows(normed, low_state)
-    grad_step_w = contract_rows(normed, low_step)
+    grad_small_w = jnp.concatenate(
+        [
+            contract_rows(normed_rows, own_state),
+            contract_rows(normed, low_step),
+            jnp.zeros((normed.shape[1], tail), jnp.float32),
+        ],
+        axis=1,
+    )
     summed = times_transposed(low_gate, gate_w)
     summed = summed + times_transposed(low_values, values_w)
-    head_part = lax.psum_scatter(
-        summed + times_transposed(low_step, step_w), "tensor", scatter_dimension=0, tiled=True
-    )
-    own_state = lax.dynamic_slice_in_dim(
-        low_state, lax.axis_index("tensor") * local_rows, local_rows, 0
+    head_part = summed + times_transposed(low_step, step_w)
+    head_part, owned_gate, owned_values, owned_output, owned_small = exchange(
+        3,
+        ("scatter", "tensor", head_part.astype(jnp.bfloat16)),
+        ("scatter", "dp", grad_gate_w.astype(jnp.bfloat16)),
+        ("scatter", "dp", grad_values_w.astype(jnp.bfloat16)),
+        ("scatter", "dp", grad_output_w.astype(jnp.bfloat16)),
+        ("scatter", "dp", grad_small_w.astype(jnp.bfloat16)),
     )
     grad_normed_rows = head_part + times_transposed(own_state, state_w)
     scaled_in = grad_normed_rows * input_gain
@@ -211,45 +360,66 @@
         - rows_in * (inv_rms * inv_rms * inv_rms) * cross_in
     ).astype(jnp.bfloat16)
     grad_gain_part = jnp.sum(grad_normed_rows * rows_in * inv_rms, axis=0)
-    grad_gain_rows = lax.psum(grad_gain_part, "tensor")
-    owned = (
-        lax.psum_scatter(grad_gate_w, "dp", scatter_dimension=0, tiled=True),
-        lax.psum_scatter(grad_values_w, "dp", scatter_dimension=0, tiled=True),
-        lax.psum_scatter(grad_state_w, "dp", scatter_dimension=0, tiled=True),
-        lax.psum_scatter(grad_step_w, "dp", scatter_dimension=0, tiled=True),
-        lax.psum_scatter(grad_output_w, "dp", scatter_dimension=0, tiled=True),
-    )
-    totals = lax.psum(
-        (
-            grad_gain_rows,
-            grad_conv_values,
-            grad_bias_values,
-            grad_conv_state,
-            grad_bias_state,
-            grad_step_bias,
-            grad_decay_log,
-            grad_skip_gain,
-            grad_mixer_gain,
-        ),
-        "dp",
-    )
+    width = grad_gain_part.shape[0]
+    channels = grad_bias_values.shape[0]
+
+    def packed(parts, columns):
+        flat = jnp.concatenate([part.reshape(-1) for part in parts])
+        filled = -(-flat.shape[0] // (8 * columns)) * 8 * columns
+        return jnp.pad(flat, (0, filled - flat.shape[0])).reshape(-1, columns)
+
+    def unpacked(table, parts):
+        flat, start, out = table.reshape(-1), 0, []
+        for part in parts:
+            out.append(flat[start : start + part.size].reshape(part.shape))
+            start += part.size
+        return out
+
+    shared = [grad_gain_part, grad_conv_part, grad_shift_part]
+    shared_sum, owned_state = exchange(
+        4,
+        ("sum", "tensor", packed(shared, width)),
+        ("sum", "tensor", owned_small[:, :state_columns]),
+    )
+    own = [
+        grad_conv_values,
+        grad_bias_values,
+        grad_mixer_gain,
+        grad_step_bias,
+        grad_decay_log,
+        grad_skip_gain,
+    ]
+    shared_sum, own_sum = exchange(
+        5,
+        ("sum", "dp", shared_sum),
+        ("sum", "dp", packed(own, channels)),
+    )
+    grad_gain, grad_conv_state, grad_bias_state = unpacked(shared_sum, shared)
+    (
+        grad_conv_values,
+        grad_bias_values,
+        grad_mixer_gain,
+        grad_step_bias,
+        grad_decay_log,
+        grad_skip_gain,
+    ) = unpacked(own_sum, own)
     return (
         layer_output,
         input_grad,
-        totals[0],
-        owned[0],
-        owned[1],
-        owned[2],
-        owned[3],
-        totals[1],
-        totals[2],
-        totals[3],
-        totals[4],
-        totals[5],
-        totals[6],
-        totals[7],
-        totals[8],
-        owned[4],
+        grad_gain,
+        owned_gate,
+        owned_values,
+        owned_state,
+        owned_small[:, state_columns : state_columns + head_count],
+        grad_conv_values,
+        grad_bias_values,
+        grad_conv_state,
+        grad_bias_state,
+        grad_step_bias,
+        grad_decay_log,
+        grad_skip_gain,
+        grad_mixer_gain,
+        owned_output,
     )
 
 

time: 712 us -> 545 us (0.77)
  waiting for transfers between devices: 281 us -> 1.4 us
  Pallas kernels: 0 us -> 145 us
  blocking collectives: 140 us -> 0 us
  local copies, waits for them, and re-layouts: 65.2 us -> 105 us
  other arithmetic: 76.4 us -> 115 us
  matrix products: 124 us -> 154 us
    reduce_scatter x6 -> x0, waiting for transfers between devices: 175 us -> none  [the longest x1 45.3 us: on_device(): lax.psum_scatter(grad_values_w, 'dp', scatter_dimension=0, tiled=True)]
    pallas_call x0 -> x6, Pallas kernels: none -> 145 us  [exchange(): pl.pallas_call(partial(exchange_kernel, tuple(plan), sizes), out_shape=tu...]
    psum x5 -> x0, blocking collectives: 120 us -> none  [the longest x1 76.4 us: on_device(): lax.psum((grad_state_part, grad_conv_part, grad_shift_part), 'tensor')]
    all_gather x4 -> x1, waiting for transfers between devices: 55.6 us -> 0.01 us  [on_device(): output_w = lax.all_gather(proj_output, 'dp', axis=0, tiled=True)]
    reduce_scatter x1, waiting for transfers between devices: 47.4 us -> 0.01 us  [on_device(): lax.psum_scatter(times_transposed(normed_out, output_w), 'tensor', scatte...]
    another operation x37 -> x39, other arithmetic: 25.1 us -> 45.9 us
    all_gather x2 -> x0, blocking collectives: 19.2 us -> none  [the longest x1 9.84 us: on_device(): lax.all_gather(proj_state, 'dp', axis=0, tiled=True)]
    dot_general x12, matrix products: 34.6 us -> 47.4 us  [block_scan(): inside = jnp.einsum('ijh,jhp->ihp', weights, scaled, precision=HIGHEST)]
  transfers between devices with their start and end apart: 12 -> 3, of which waited for: 9 -> 0; matrix products, arithmetic and copies ran while one was open for 36% -> 63% of each run, Pallas kernels for 0% -> 26%
where the time goes in v1:
time: 545 us; the launch traced here: 536 us
  matrix products  154 us (28%)
  Pallas kernels  145 us (27%)
  other arithmetic  115 us (21%)
  local copies, waits for them, and re-layouts  105 us (19%)
  between operations  15.6 us (3%)
    pallas_call x6, Pallas kernels, exchange(): pl.pallas_call(partial(exchange_kernel, tuple(plan), sizes), out_shape=tu...  145 us
    dot_general x12, matrix products, block_scan(): inside = jnp.einsum('ijh,jhp->ihp', weights, scaled, precision=HIGHEST)  47.4 us
    another operation x38, other arithmetic  45.9 us
    dot_general x16, matrix products, block_scan(): jnp.einsum('in,hpn->ihp', output_map, carry_state, precision=HIGHEST)  31.1 us
    squeeze x16, local copies, waits for them, and re-layouts, mixer_core(): lax.scan(jax.checkpoint(partial(block_scan, decay_rate=decay_rate)), init...  24.4 us
    dot_general x16, matrix products, block_scan(): scores = jnp.dot(output_map, input_map.T, precision=HIGHEST)  23.5 us
    dot_general x12, matrix products, block_scan(): jnp.einsum('jhp,jn->hpn', scaled * remain[:, :, None], input_map, precisi...  21 us
    another operation x29, local copies, waits for them, and re-layouts  16.6 us
  transfers between devices with their start and end apart: 3, of which 0 were waited for; matrix products, arithmetic and copies ran while one was open for 63% of the time, Pallas kernels for 26%

profile of v1, /device:TPU:9, one launch (start us, length us, event | category | flops | bytes accessed | tf_op | source)
XLA Modules:
  0.0 536.1 jit_solution(9980208293722798049)
XLA Ops:
  15.7 50.5 %shard_map.288 = (bf16[1024,1024]{1,0:T(8,128)(2,1)S(1)}, bf16[1024,512]{1,0:T(8,128)(2,1)S(1)}, bf16[1024,512]{1,0:T(8,128)(2,1)S(1)}, bf16[1024,384]{1,0:T(8,128)(2,1)S(1)}) custom-call(bf16[256,1024]{1,0:T(8,128)(2,1)S(1)} %fusion.101.refs_0_, bf16[128,512]{1,0:T(8,128)(2,1)S(1)} %copy-done.2, bf16[128,512]{1,0:T(8,128)(2,1)S(1)} %copy-done.3, ...), custom_call_target="tpu_custom_call" | custom-call | tf_op jit(solution)/shard_map/pallas_call | solution.py:205
  71.1 3.4 subtract_add_fusion.16
  74.6 4.6 reshape.426
  79.1 3.9 copy.144
  87.1 46.8 %while.41 = (s32[]{:T(128)}, f32[8,64,128]{2,1,0:T(8,128)S(1)}, f32[4,256,8,64]{1,3,2,0:T(8,128)}, f32[4,8,64,128]{3,2,1,0:T(8,128)}, f32[4,256,8]{1,2,0:T(8,128...) while((s32[]{:T(128)}, f32[8,64,128]{2,1,0:T(8,128)S(1)}, ...), condition=%wide.region_4.5_spmd.clone, body=%wide.region_1.4_spmd.clone.sunk | while | flops 911937536 | bytes 5182293 | solution.py:84
  90.1 3.7 fusion.220
  93.7 2.3 fusion.221
  101.8 3.7 fusion.220
  105.4 2.3 fusion.221
  113.5 3.7 fusion.220
  117.2 2.3 fusion.221
  125.2 3.7 fusion.220
  128.8 2.3 fusion.221
  133.9 3.8 copy.158
  137.7 4.8 reshape.423
  142.6 3.8 fusion.142
  146.5 6.3 %multiply_reduce_fusion.11 = (f32[1024]{0:T(1024)S(1)}, f32[1024]{0:T(1024)S(1)}, f32[1024,512]{1,0:T(8,128)S(1)}, f32[1024,512]{1,0:T(8,128)S(1)}) fusion(f32[512]{0:T(512)S(1)} %copy-done.39, f32[1024,512]{1,0:T(8,128)} %fusion.142, f32[1024]{0:T(1024)S(1)} %fusion.125, f32[1024,512]{1,0:T(8,128)} %reshape.423, f32[1024,512]{1,0:T(8,128)} %get-tuple-element.875, ...), kind=kOutput, calls=%fused_computation.163 | convolution fusion | flops 1084749824 | bytes 13647872 | tf_op jit(solution)/shard_map/dot_general | solution.py:297
  152.9 4.2 shard_map.289
  157.1 4.4 multiply_reduce_fusion.4
  161.5 4.4 reshape.424
  165.9 4.2 copy.149
  170.1 5.1 fusion.127
  179.0 213.0 %while.42 = (s32[]{:T(128)}, f32[8]{0:T(128)}, f32[8,64,128]{2,1,0:T(8,128)}, f32[4,256,8,64]{1,3,2,0:T(8,128)}, f32[4,256,8]{1,2,0:T(8,128)}, /*index=5*/f32[4,...) while((s32[]{:T(128)}, f32[8]{0:T(128)}, ...), condition=%wide.region_22.23_spmd.clone, body=%wide.region_8.22_spmd.clone.sunk | while | flops 2126804992 | bytes 23833500 | solution.py:84
  194.6 4.7 fusion.240
  206.0 2.2 fusion.245
  209.7 3.5 multiply_reduce_fusion.20
  218.7 3.2 reduce-window.74
  247.6 4.8 fusion.240
  259.1 2.2 fusion.245
  262.8 3.5 multiply_reduce_fusion.20
  271.8 3.2 reduce-window.74
  301.2 4.7 fusion.240
  312.7 2.2 fusion.245
  316.4 3.5 multiply_reduce_fusion.20
  325.4 3.2 reduce-window.74
  354.8 4.7 fusion.240
  370.0 3.5 multiply_reduce_fusion.20
  379.0 3.2 reduce-window.74
  392.0 4.0 copy.161
  396.0 4.8 reshape.425
  400.9 3.7 multiply_reduce_fusion.15
  405.3 14.4 %shard_map.290 = f32[256,256]{1,0:T(8,128)S(1)} custom-call(bf16[1024,256]{1,0:T(8,128)(2,1)S(1)} %fusion.109.refs_0_), custom_call_target="tpu_custom_call" | custom-call | tf_op jit(solution)/shard_map/pallas_call | solution.py:205
  420.5 6.6 %multiply_reduce_fusion.9 = (f32[512]{0:T(512)S(1)}, f32[512]{0:T(512)S(1)}, f32[512]{0:T(512)S(1)}, f32[512]{0:T(512)S(1)}, f32[512]{0:T(512)S(1)}, /*index=5*/f32[1024,512]{1,0:T(8,128)S(1)}) fusion(f32[1024,512]{1,0:T(8,128)} %copy-done.16, f32[1024,512]{1,0:T(8,128)} %get-tuple-element.875, f32[1024,512]{1,0:T(8,128)} %reshape.425, ...), kind=kLoop, calls=%fused_computation.158 | loop fusion | flops 10483200 | bytes 10498048 | tf_op jit(solution)/shard_map/transpose(jvp())/reduce_sum | solution.py:28
  439.9 49.3 %shard_map.291 = (f32[256,1024]{1,0:T(8,128)S(1)}, f32[128,512]{1,0:T(8,128)S(1)}, f32[128,512]{1,0:T(8,128)S(1)}, f32[128,512]{1,0:T(8,128)S(1)}, f32[128,384]{1,0:T(8,128)S(1)}) custom-call(bf16[1024,1024]{1,0:T(8,128)(2,1)} %add_convert_fusion.refs_0_, bf16[1024,512]{1,0:T(8,128)(2,1)S(1)} %convolution_convert_fusion.2.refs_1_, ...), custom_call_target="tpu_custom_call" | custom-call | tf_op jit(solution)/shard_map/pallas_call | solution.py:205
  490.4 2.5 fusion.108
  492.9 18.7 %shard_map.292 = (f32[8,1024]{1,0:T(8,128)S(1)}, f32[128,256]{1,0:T(8,128)S(1)}) custom-call(f32[8,1024]{1,0:T(8,128)S(1)} %reshape.400.refs_0_, f32[128,256]{1,0:T(8,128)S(1)} %slice.192.refs_1_), custom_call_target="tpu_custom_call" | custom-call | tf_op jit(solution)/shard_map/pallas_call | solution.py:205
  511.6 7.5 %shard_map.293 = (f32[8,1024]{1,0:T(8,128)S(1)}, f32[8,512]{1,0:T(8,128)S(1)}) custom-call(f32[8,1024]{1,0:T(8,128)S(1)} %get-tuple-element.415.refs_0_, f32[8,512]{1,0:T(8,128)S(1)} %reshape.406.refs_1_), custom_call_target="tpu_custom_call" | custom-call | tf_op jit(solution)/shard_map/pallas_call | solution.py:205
  523.4 3.2 fusion.105
  (488 shorter events, 225.9 us)
Async XLA Ops:
  7.2 7.6 %copy-start.36 = (bf16[128,256]{1,0:T(8,128)(2,1)S(1)}, bf16[128,256]{1,0:T(8,128)(2,1)}, u32[]{:S(2)}) copy-start(bf16[128,256]{1,0:T(8,128)(2,1)} %param.26) | copy-start | bytes 196612
  7.2 7.6 %copy-start.2 = (bf16[128,512]{1,0:T(8,128)(2,1)S(1)}, bf16[128,512]{1,0:T(8,128)(2,1)}, u32[]{:S(2)}) copy-start(bf16[128,512]{1,0:T(8,128)(2,1)} %refs_1_.1) | copy-start | bytes 393220
  7.2 139.3 %all-gather.5.cloned.1.call-start = ((), (), s32[]{:S(2)}) async-start(), calls=%async_computation.2 | async-start | bytes 1179648 | tf_op jit(solution)/shard_map/all_gather | solution.py:275
  7.9 138.6 %all-gather.3.cloned.1.call-start = ((), (), s32[]{:S(2)}) async-start(), calls=%async_computation.1 | async-start | bytes 2621440 | tf_op jit(solution)/shard_map/all_gather | solution.py:276
  8.7 514.7 %reduce-scatter.2.cloned.1.call-start = ((), (), s32[]{:S(2)}) async-start(), calls=%async_computation.3 | async-start | bytes 5242880 | tf_op jit(solution)/shard_map/reduce_scatter | solution.py:306
  12.9 54.1 %copy-start.53 = (f32[1,256]{1,0:T(1,128)}, f32[1,256]{1,0:T(1,128)S(1)}, u32[]{:S(2)}) copy-start(f32[1,256]{1,0:T(1,128)S(1)} %get-tuple-element.910) | copy-start | bytes 3076
  12.9 54.1 %copy-start.55 = (f32[1,256]{1,0:T(1,128)}, f32[1,256]{1,0:T(1,128)S(1)}, u32[]{:S(2)}) copy-start(f32[1,256]{1,0:T(1,128)S(1)} %get-tuple-element.911) | copy-start | bytes 3076
  12.9 54.1 %copy-start.57 = (f32[1,256]{1,0:T(1,128)}, f32[1,256]{1,0:T(1,128)S(1)}, u32[]{:S(2)}) copy-start(f32[1,256]{1,0:T(1,128)S(1)} %get-tuple-element.912) | copy-start | bytes 3076
  12.9 54.1 %copy-start.59 = (f32[1,256]{1,0:T(1,128)}, f32[1,256]{1,0:T(1,128)S(1)}, u32[]{:S(2)}) copy-start(f32[1,256]{1,0:T(1,128)S(1)} %get-tuple-element.913) | copy-start | bytes 3076
  66.2 18.0 %copy-start = (bf16[1024,384]{1,0:T(8,128)(2,1)}, bf16[1024,384]{1,0:T(8,128)(2,1)S(1)}, u32[]{:S(2)}) copy-start(bf16[1024,384]{1,0:T(8,128)(2,1)S(1)} %get-tuple-element.404) | copy-start | bytes 2359300
  83.7 73.4 %copy-start.34 = (f32[1024]{0:T(1024)}, f32[1024]{0:T(1024)S(1)}, u32[]{:S(2)}) copy-start(f32[1024]{0:T(1024)S(1)} %fusion.125) | copy-start | bytes 12292
  142.6 14.5 %copy-start.49 = (f32[512]{0:T(512)}, f32[512]{0:T(512)S(1)}, u32[]{:S(2)}) copy-start(f32[512]{0:T(512)S(1)} %mul.807) | copy-start | bytes 6148
  146.5 10.6 %copy-start.13 = (f32[1024,512]{1,0:T(8,128)S(1)}, f32[1024,512]{1,0:T(8,128)}, u32[]{:S(2)}) copy-start(f32[1024,512]{1,0:T(8,128)} %get-tuple-element.875) | copy-start | bytes 6291460
  146.5 10.6 %copy-start.17 = (f32[1024,512]{1,0:T(8,128)S(1)}, f32[1024,512]{1,0:T(8,128)}, u32[]{:S(2)}) copy-start(f32[1024,512]{1,0:T(8,128)} %reshape.423) | copy-start | bytes 6291460
  146.5 10.6 %copy-start.21 = (f32[1024,512]{1,0:T(8,128)S(1)}, f32[1024,512]{1,0:T(8,128)}, u32[]{:S(2)}) copy-start(f32[1024,512]{1,0:T(8,128)} %fusion.142) | copy-start | bytes 6291460
  152.8 8.7 %copy-start.14 = (f32[1024,512]{1,0:T(8,128)}, f32[1024,512]{1,0:T(8,128)S(1)}, u32[]{:S(2)}) copy-start(f32[1024,512]{1,0:T(8,128)S(1)} %get-tuple-element.871) | copy-start | bytes 6291460
  157.1 13.0 %copy-start.30 = (f32[1,1024]{1,0:T(1,128)}, f32[1,1024]{1,0:T(1,128)S(1)}, u32[]{:S(2)}) copy-start(f32[1,1024]{1,0:T(1,128)S(1)} %get-tuple-element.900) | copy-start | bytes 12292
  202.3 7.4 %copy-start.10 = (f32[256,8,64]{0,2,1:T(8,128)S(1)}, f32[256,8,64]{0,2,1:T(8,128)}, u32[]{:S(2)}) copy-start(f32[256,8,64]{0,2,1:T(8,128)} %get-tuple-element.1109) | copy-start | bytes 1572868 | tf_op jit(solution)/shard_map/transpose(jvp())/while
  202.3 7.4 %copy-start.19 = (f32[256,256]{1,0:T(8,128)S(1)}, f32[256,256]{1,0:T(8,128)}, u32[]{:S(2)}) copy-start(f32[256,256]{1,0:T(8,128)} %copy-done.18) | copy-start | bytes 786436 | tf_op jit(solution)/shard_map/transpose(jvp())/while
  202.3 7.4 %copy-start.26 = (pred[256,256]{1,0:T(8,128)(4,1)S(1)}, pred[256,256]{1,0:T(8,128)(4,1)}, u32[]{:S(2)}) copy-start(pred[256,256]{1,0:T(8,128)(4,1)} %copy-done.25) | copy-start | bytes 196612 | tf_op jit(solution)/shard_map/transpose(jvp())/while
  203.9 9.3 %copy-start.29 = (f32[8]{0:T(128)}, f32[8]{0:T(128)S(1)}, u32[]{:S(2)}) copy-start(f32[8]{0:T(128)S(1)} %get-tuple-element.1115) | copy-start | bytes 100 | tf_op jit(solution)/shard_map/transpose(jvp())/while
  247.6 5.8 %copy-start.8 = (f32[8,64,128]{2,1,0:T(8,128)S(1)}, f32[8,64,128]{2,1,0:T(8,128)}, u32[]{:S(2)}) copy-start(f32[8,64,128]{2,1,0:T(8,128)} %dynamic-slice_bitcast_fusion.12) | copy-start | bytes 786436 | tf_op jit(solution)/shard_map/transpose(jvp())/while
  255.4 7.4 %copy-start.10 = (f32[256,8,64]{0,2,1:T(8,128)S(1)}, f32[256,8,64]{0,2,1:T(8,128)}, u32[]{:S(2)}) copy-start(f32[256,8,64]{0,2,1:T(8,128)} %get-tuple-element.1109) | copy-start | bytes 1572868 | tf_op jit(solution)/shard_map/transpose(jvp())/while
  255.4 7.4 %copy-start.19 = (f32[256,256]{1,0:T(8,128)S(1)}, f32[256,256]{1,0:T(8,128)}, u32[]{:S(2)}) copy-start(f32[256,256]{1,0:T(8,128)} %copy-done.18) | copy-start | bytes 786436 | tf_op jit(solution)/shard_map/transpose(jvp())/while
  255.4 7.4 %copy-start.26 = (pred[256,256]{1,0:T(8,128)(4,1)S(1)}, pred[256,256]{1,0:T(8,128)(4,1)}, u32[]{:S(2)}) copy-start(pred[256,256]{1,0:T(8,128)(4,1)} %copy-done.25) | copy-start | bytes 196612 | tf_op jit(solution)/shard_map/transpose(jvp())/while
  256.9 9.3 %copy-start.29 = (f32[8]{0:T(128)}, f32[8]{0:T(128)S(1)}, u32[]{:S(2)}) copy-start(f32[8]{0:T(128)S(1)} %get-tuple-element.1115) | copy-start | bytes 100 | tf_op jit(solution)/shard_map/transpose(jvp())/while
  309.0 7.4 %copy-start.10 = (f32[256,8,64]{0,2,1:T(8,128)S(1)}, f32[256,8,64]{0,2,1:T(8,128)}, u32[]{:S(2)}) copy-start(f32[256,8,64]{0,2,1:T(8,128)} %get-tuple-element.1109) | copy-start | bytes 1572868 | tf_op jit(solution)/shard_map/transpose(jvp())/while
  309.0 7.4 %copy-start.19 = (f32[256,256]{1,0:T(8,128)S(1)}, f32[256,256]{1,0:T(8,128)}, u32[]{:S(2)}) copy-start(f32[256,256]{1,0:T(8,128)} %copy-done.18) | copy-start | bytes 786436 | tf_op jit(solution)/shard_map/transpose(jvp())/while
  309.0 7.4 %copy-start.26 = (pred[256,256]{1,0:T(8,128)(4,1)S(1)}, pred[256,256]{1,0:T(8,128)(4,1)}, u32[]{:S(2)}) copy-start(pred[256,256]{1,0:T(8,128)(4,1)} %copy-done.25) | copy-start | bytes 196612 | tf_op jit(solution)/shard_map/transpose(jvp())/while
  310.5 9.3 %copy-start.29 = (f32[8]{0:T(128)}, f32[8]{0:T(128)S(1)}, u32[]{:S(2)}) copy-start(f32[8]{0:T(128)S(1)} %get-tuple-element.1115) | copy-start | bytes 100 | tf_op jit(solution)/shard_map/transpose(jvp())/while
  362.6 7.4 %copy-start.10 = (f32[256,8,64]{0,2,1:T(8,128)S(1)}, f32[256,8,64]{0,2,1:T(8,128)}, u32[]{:S(2)}) copy-start(f32[256,8,64]{0,2,1:T(8,128)} %get-tuple-element.1109) | copy-start | bytes 1572868 | tf_op jit(solution)/shard_map/transpose(jvp())/while
  362.6 7.4 %copy-start.19 = (f32[256,256]{1,0:T(8,128)S(1)}, f32[256,256]{1,0:T(8,128)}, u32[]{:S(2)}) copy-start(f32[256,256]{1,0:T(8,128)} %copy-done.18) | copy-start | bytes 786436 | tf_op jit(solution)/shard_map/transpose(jvp())/while
  362.6 7.4 %copy-start.26 = (pred[256,256]{1,0:T(8,128)(4,1)S(1)}, pred[256,256]{1,0:T(8,128)(4,1)}, u32[]{:S(2)}) copy-start(pred[256,256]{1,0:T(8,128)(4,1)} %copy-done.25) | copy-start | bytes 196612 | tf_op jit(solution)/shard_map/transpose(jvp())/while
  364.2 9.3 %copy-start.29 = (f32[8]{0:T(128)}, f32[8]{0:T(128)S(1)}, u32[]{:S(2)}) copy-start(f32[8]{0:T(128)S(1)} %get-tuple-element.1115) | copy-start | bytes 100 | tf_op jit(solution)/shard_map/transpose(jvp())/while
  404.9 14.8 %copy-start.32 = (f32[1024,8]{0,1:T(8,128)S(1)}, f32[1024,8]{0,1:T(8,128)}, u32[]{:S(2)}) copy-start(f32[1024,8]{0,1:T(8,128)} %get-tuple-element.919) | copy-start | bytes 98308
  405.0 14.8 %copy-start.33 = (f32[4,256,8]{1,2,0:T(8,128)S(1)}, f32[4,256,8]{1,2,0:T(8,128)}, u32[]{:S(2)}) copy-start(f32[4,256,8]{1,2,0:T(8,128)} %get-tuple-element.410) | copy-start | bytes 98308
  405.0 14.8 %copy-start.35 = (f32[1024]{0:T(1024)S(1)}, f32[1024]{0:T(1024)}, u32[]{:S(2)}) copy-start(f32[1024]{0:T(1024)} %copy-done.34) | copy-start | bytes 12292
  405.3 15.1 %copy-start.50 = (f32[512]{0:T(512)S(1)}, f32[512]{0:T(512)}, u32[]{:S(2)}) copy-start(f32[512]{0:T(512)} %copy-done.49) | copy-start | bytes 6148
  420.5 6.6 %copy-start.42 = (f32[1,512]{1,0:T(1,128)S(1)}, f32[1,512]{1,0:T(1,128)}, u32[]{:S(2)}) copy-start(f32[1,512]{1,0:T(1,128)} %copy-done.41) | copy-start | bytes 6148
  420.5 6.6 %copy-start.44 = (f32[1,512]{1,0:T(1,128)S(1)}, f32[1,512]{1,0:T(1,128)}, u32[]{:S(2)}) copy-start(f32[1,512]{1,0:T(1,128)} %copy-done.43) | copy-start | bytes 6148
  420.5 6.6 %copy-start.46 = (f32[1,512]{1,0:T(1,128)S(1)}, f32[1,512]{1,0:T(1,128)}, u32[]{:S(2)}) copy-start(f32[1,512]{1,0:T(1,128)} %copy-done.45) | copy-start | bytes 6148
  420.5 6.6 %copy-start.48 = (f32[1,512]{1,0:T(1,128)S(1)}, f32[1,512]{1,0:T(1,128)}, u32[]{:S(2)}) copy-start(f32[1,512]{1,0:T(1,128)} %copy-done.47) | copy-start | bytes 6148
  439.9 49.4 %copy-start.63 = (f32[512]{0:T(512)S(1)}, f32[512]{0:T(512)}, u32[]{:S(2)}) copy-start(f32[512]{0:T(512)} %get-tuple-element.865) | copy-start | bytes 6148
  439.9 49.6 %copy-start.73 = (f32[8]{0:T(128)S(1)}, f32[8]{0:T(128)}, u32[]{:S(2)}) copy-start(f32[8]{0:T(128)} %param.33) | copy-start | bytes 100
  439.9 50.3 %copy-start.64 = (f32[512]{0:T(512)S(1)}, f32[512]{0:T(512)}, u32[]{:S(2)}) copy-start(f32[512]{0:T(512)} %get-tuple-element.884) | copy-start | bytes 6148
  439.9 50.4 %copy-start.38 = (f32[1024]{0:T(1024)S(1)}, f32[1024]{0:T(1024)}, u32[]{:S(2)}) copy-start(f32[1024]{0:T(1024)} %param.23) | copy-start | bytes 12292
  439.9 50.4 %copy-start.52 = (f32[256]{0:T(256)S(1)}, f32[256]{0:T(256)}, u32[]{:S(2)}) copy-start(f32[256]{0:T(256)} %copy-done.51) | copy-start | bytes 3076
  489.3 34.1 %copy-start.66 = (f32[256]{0:T(256)S(1)}, f32[256]{0:T(256)}, u32[]{:S(2)}) copy-start(f32[256]{0:T(256)} %get-tuple-element.914) | copy-start | bytes 3076
  (65 other events, 198.0 us)
Sparse Core Ops, SparseCore 0:
  9.9 43.6 all-gather.4
  55.1 45.5 all-gather.2
  175.3 78.7 reduce-scatter.1

commit v2 on v1

--- a/solution.py
+++ b/solution.py
@@ -29,29 +29,194 @@
     return summed
 
 
-def block_scan(carry_state, pieces, decay_rate):
-    values, step_sizes, input_map, output_map = pieces
-    logdecay = jnp.cumsum(step_sizes * decay_rate, axis=0)
-    spread = logdecay[:, None, :] - logdecay[None, :, :]
-    causal = (jnp.arange(BLOCK)[:, None] >= jnp.arange(BLOCK)[None, :])[:, :, None]
-    decays = jnp.exp(jnp.where(causal, spread, -10000.0))
-    scores = jnp.dot(output_map, input_map.T, precision=HIGHEST)
-    weights = rounded(scores[:, :, None] * decays)
-    scaled = rounded(values * step_sizes[:, :, None])
-    inside = jnp.einsum("ijh,jhp->ihp", weights, scaled, precision=HIGHEST)
-    carried = (
-        jnp.einsum("in,hpn->ihp", output_map, carry_state, precision=HIGHEST)
-        * jnp.exp(logdecay)[:, :, None]
-    )
-    remain = jnp.exp(logdecay[-1][None, :] - logdecay)
-    new_state = carry_state * jnp.exp(logdecay[-1])[:, None, None] + jnp.einsum(
-        "jhp,jn->hpn", scaled * remain[:, :, None], input_map, precision=HIGHEST
-    )
-    return (new_state, inside + carried)
-
-
-def mixer_core(
-    gate_in,
+def rows_by_rows(left_side, right_side):
+    return lax.dot_general(
+        left_side, right_side, (((0,), (0,)), ((), ())), preferred_element_type=jnp.float32
+    )
+
+
+def columns_by_columns(left_side, right_side):
+    return lax.dot_general(
+        left_side, right_side, (((1,), (1,)), ((), ())), preferred_element_type=jnp.float32
+    )
+
+
+def causal_mask(length):
+    return lax.broadcasted_iota(jnp.int32, (length, length), 0) >= lax.broadcasted_iota(
+        jnp.int32, (length, length), 1
+    )
+
+
+def forward_kernel(values_ref, maps_ref, step_ref, cum_ref, across_ref, out_ref, kept_ref, state):
+    heads = step_ref.shape[1]
+    length, channels = values_ref.shape
+    dim = channels // heads
+    width = maps_ref.shape[1] // 2
+
+    @pl.when(pl.program_id(0) == 0)
+    def _():
+        state[...] = jnp.zeros_like(state)
+
+    kept_ref[0] = state[...]
+    input_map, output_map = maps_ref[:, :width], maps_ref[:, width:]
+    scores = columns_by_columns(output_map, input_map)
+    carried = columns_by_columns(output_map, state[...].astype(jnp.bfloat16))
+    mask = causal_mask(length)
+    remains = []
+    for head in range(heads):
+        part = slice(head * dim, (head + 1) * dim)
+        cum = cum_ref[:, head : head + 1]
+        across = across_ref[head : head + 1, :]
+        decays = jnp.exp(jnp.where(mask, cum - across, -10000.0))
+        weights = (scores * decays).astype(jnp.bfloat16)
+        scaled = (values_ref[:, part].astype(jnp.float32) * step_ref[:, head : head + 1]).astype(
+            jnp.bfloat16
+        )
+        inside = jnp.dot(weights, scaled, preferred_element_type=jnp.float32)
+        out_ref[:, part] = inside + carried[:, part] * jnp.exp(cum)
+        last = across[:, length - 1 : length]
+        remains.append((scaled.astype(jnp.float32) * jnp.exp(last - cum)).astype(jnp.bfloat16))
+        state[part, :] = state[part, :] * jnp.exp(last)
+    state[...] += rows_by_rows(jnp.concatenate(remains, axis=1), input_map)
+
+
+def backward_kernel(
+    values_ref, maps_ref, step_ref, cum_ref, across_ref, kept_ref, grad_ref,
+    grad_values_ref, grad_maps_ref, grad_step_ref, grad_cum_ref, grad_across_ref, grad_state,
+):
+    heads = step_ref.shape[1]
+    length, channels = values_ref.shape
+    dim = channels // heads
+    width = maps_ref.shape[1] // 2
+
+    @pl.when(pl.program_id(0) == 0)
+    def _():
+        grad_state[...] = jnp.zeros_like(grad_state)
+
+    input_map, output_map = maps_ref[:, :width], maps_ref[:, width:]
+    scores = columns_by_columns(output_map, input_map)
+    kept = kept_ref[0].astype(jnp.bfloat16)
+    low_state = grad_state[...].astype(jnp.bfloat16)
+    carried = columns_by_columns(output_map, kept)
+    pulled = columns_by_columns(input_map, low_state)
+    mask = causal_mask(length)
+    is_last = lax.broadcasted_iota(jnp.int32, (1, length), 1) == length - 1
+    grad_scores = jnp.zeros((length, length), jnp.float32)
+    faded, remains = [], []
+    for head in range(heads):
+        part = slice(head * dim, (head + 1) * dim)
+        cum = cum_ref[:, head : head + 1]
+        across = across_ref[head : head + 1, :]
+        step = step_ref[:, head : head + 1]
+        values = values_ref[:, part].astype(jnp.float32)
+        decays = jnp.exp(jnp.where(mask, cum - across, -10000.0))
+        spread = scores * decays
+        weights = spread.astype(jnp.bfloat16)
+        scaled = (values * step).astype(jnp.bfloat16)
+        grad = grad_ref[:, part]
+        low_grad = grad.astype(jnp.bfloat16)
+        grad_weights = columns_by_columns(low_grad, scaled)
+        grad_scores += grad_weights * decays
+        product = grad_weights * spread
+        last = across[:, length - 1 : length]
+        remain = jnp.exp(last - cum)
+        kept_scaled = scaled.astype(jnp.float32) * remain
+        grad_remain = jnp.sum(kept_scaled * pulled[:, part], axis=1, keepdims=True)
+        faded_grad = grad * jnp.exp(cum)
+        grad_cum_ref[:, head : head + 1] = (
+            jnp.sum(product, axis=1, keepdims=True)
+            + jnp.sum(faded_grad * carried[:, part], axis=1, keepdims=True)
+            - grad_remain
+        )
+        on_last = jnp.sum(grad_remain, axis=0, keepdims=True) + jnp.exp(last) * jnp.sum(
+            jnp.sum(kept_ref[0, part, :] * grad_state[part, :], axis=1, keepdims=True),
+            axis=0,
+            keepdims=True,
+        )
+        grad_across_ref[head : head + 1, :] = (
+            jnp.where(is_last, on_last, 0.0) - jnp.sum(product, axis=0, keepdims=True)
+        )
+        grad_scaled = rows_by_rows(weights, low_grad) + remain * pulled[:, part]
+        grad_values_ref[:, part] = grad_scaled * step
+        grad_step_ref[:, head : head + 1] = jnp.sum(grad_scaled * values, axis=1, keepdims=True)
+        faded.append(faded_grad.astype(jnp.bfloat16))
+        remains.append(kept_scaled.astype(jnp.bfloat16))
+        grad_state[part, :] = grad_state[part, :] * jnp.exp(last)
+    all_faded = jnp.concatenate(faded, axis=1)
+    all_remains = jnp.concatenate(remains, axis=1)
+    low_scores = grad_scores.astype(jnp.bfloat16)
+    grad_maps_ref[:, :width] = rows_by_rows(low_scores, output_map) + jnp.dot(
+        all_remains, low_state, preferred_element_type=jnp.float32
+    )
+    grad_maps_ref[:, width:] = jnp.dot(
+        low_scores, input_map, preferred_element_type=jnp.float32
+    ) + jnp.dot(all_faded, kept, preferred_element_type=jnp.float32)
+    grad_state[...] += rows_by_rows(all_faded, output_map)
+
+
+def scan_specs(length, channels, maps, heads, place):
+    return [
+        pl.BlockSpec((BLOCK, channels), lambda i: (place(i), 0)),
+        pl.BlockSpec((BLOCK, maps), lambda i: (place(i), 0)),
+        pl.BlockSpec((BLOCK, heads), lambda i: (place(i), 0)),
+        pl.BlockSpec((BLOCK, heads), lambda i: (place(i), 0)),
+        pl.BlockSpec((heads, BLOCK), lambda i: (0, place(i))),
+    ]
+
+
+def scan_forward(values, maps, step_sizes, cum):
+    length, channels = values.shape
+    heads, columns = step_sizes.shape[1], maps.shape[1]
+    blocks = length // BLOCK
+    return pl.pallas_call(
+        forward_kernel,
+        grid=(blocks,),
+        out_shape=(
+            jax.ShapeDtypeStruct((length, channels), jnp.float32),
+            jax.ShapeDtypeStruct((blocks, channels, columns // 2), jnp.float32),
+        ),
+        in_specs=scan_specs(length, channels, columns, heads, lambda i: i),
+        out_specs=(
+            pl.BlockSpec((BLOCK, channels), lambda i: (i, 0)),
+            pl.BlockSpec((1, channels, columns // 2), lambda i: (i, 0, 0)),
+        ),
+        scratch_shapes=[pltpu.VMEM((channels, columns // 2), jnp.float32)],
+        compiler_params=pltpu.CompilerParams(vmem_limit_bytes=24 * 2**20),
+    )(values, maps, step_sizes, cum, cum.T)
+
+
+def scan_backward(values, maps, step_sizes, cum, kept, grad):
+    length, channels = values.shape
+    heads, columns = step_sizes.shape[1], maps.shape[1]
+    blocks = length // BLOCK
+
+    def place(i):
+        return blocks - 1 - i
+
+    specs = scan_specs(length, channels, columns, heads, place)
+    grad_values, grad_maps, grad_step, grad_cum, grad_across = pl.pallas_call(
+        backward_kernel,
+        grid=(blocks,),
+        out_shape=(
+            jax.ShapeDtypeStruct((length, channels), jnp.float32),
+            jax.ShapeDtypeStruct((length, columns), jnp.float32),
+            jax.ShapeDtypeStruct((length, heads), jnp.float32),
+            jax.ShapeDtypeStruct((length, heads), jnp.float32),
+            jax.ShapeDtypeStruct((heads, length), jnp.float32),
+        ),
+        in_specs=specs
+        + [
+            pl.BlockSpec((1, channels, columns // 2), lambda i: (place(i), 0, 0)),
+            pl.BlockSpec((BLOCK, channels), lambda i: (place(i), 0)),
+        ],
+        out_specs=tuple(specs),
+        scratch_shapes=[pltpu.VMEM((channels, columns // 2), jnp.float32)],
+        compiler_params=pltpu.CompilerParams(vmem_limit_bytes=24 * 2**20),
+    )(values, maps, step_sizes, cum, cum.T, kept, grad)
+    return grad_values, grad_maps, grad_step, grad_cum + grad_across.T
+
+
+def before_scan(
     values_in,
     state_in,
     step_in,
@@ -61,32 +226,21 @@
     bias_state,
     step_bias,
     decay_log,
-    skip_gain,
     present,
 ):
-    length = values_in.shape[0]
-    head_count = step_in.shape[1]
-    head_dim = values_in.shape[1] // head_count
-    state_width = state_in.shape[1] // 2
     values = rounded(jax.nn.silu(causal_conv(values_in, conv_values, bias_values)))
-    state_maps = rounded(jax.nn.silu(causal_conv(state_in, conv_state, bias_state)))
+    maps = rounded(jax.nn.silu(causal_conv(state_in, conv_state, bias_state)))
     step_sizes = jax.nn.softplus(step_in + step_bias) * present[:, None]
-    decay_rate = -jnp.exp(decay_log)
-    blocks = length // BLOCK
-    head_values = values.reshape(length, head_count, head_dim)
-    pieces = (
-        head_values.reshape(blocks, BLOCK, head_count, head_dim),
-        step_sizes.reshape(blocks, BLOCK, head_count),
-        state_maps[:, :state_width].reshape(blocks, BLOCK, state_width),
-        state_maps[:, state_width:].reshape(blocks, BLOCK, state_width),
-    )
-    initial = jnp.zeros((head_count, head_dim, state_width), jnp.float32)
-    _, outputs = lax.scan(
-        jax.checkpoint(partial(block_scan, decay_rate=decay_rate)), initial, pieces
-    )
-    mixed = outputs.reshape(length, head_count, head_dim) + skip_gain[None, :, None] * head_values
-    mixed = mixed.reshape(length, head_count * head_dim) * present[:, None]
-    return mixed * jax.nn.silu(gate_in)
+    length, heads = step_sizes.shape
+    changes = (step_sizes * -jnp.exp(decay_log)).reshape(length // BLOCK, BLOCK, heads)
+    lower = causal_mask(BLOCK).astype(jnp.float32)
+    cum = jnp.einsum("ij,bjh->bih", lower, changes, precision=HIGHEST)
+    return values, maps, step_sizes, cum.reshape(length, heads)
+
+
+def after_scan(scanned, values, gate_in, skip_gain, present):
+    skip = jnp.repeat(skip_gain, values.shape[1] // skip_gain.shape[0])
+    return (scanned + skip * values) * present[:, None] * jax.nn.silu(gate_in)
 
 
 def exchange_kernel(plan, sizes, *refs):
@@ -213,7 +367,7 @@
             pltpu.SemaphoreType.DMA((len(items), most)),
         ],
         compiler_params=pltpu.CompilerParams(
-            collective_id=identity, has_side_effects=True, vmem_limit_bytes=48 * 2**20
+            collective_id=identity, has_side_effects=True, vmem_limit_bytes=24 * 2**20
         ),
     )(*[array for _, _, array in items])
 
@@ -279,10 +433,8 @@
     state_in = project(normed, state_w)
     step_in = project(normed, step_w)
     present = (jnp.arange(normed.shape[0]) < lengths[0]).astype(jnp.float32)
-    core = partial(mixer_core, present=present)
-    gated, core_pull = jax.vjp(
-        core,
-        gate_in,
+    (values, maps, step_sizes, cum), before_pull = jax.vjp(
+        partial(before_scan, present=present),
         values_in,
         state_in,
         step_in,
@@ -292,7 +444,11 @@
         bias_state,
         step_bias,
         decay_log,
-        skip_gain,
+    )
+    low_values, low_maps = values.astype(jnp.bfloat16), maps.astype(jnp.bfloat16)
+    scanned, kept = scan_forward(low_values, low_maps, step_sizes, cum)
+    gated, after_pull = jax.vjp(
+        partial(after_scan, present=present), scanned, values, gate_in, skip_gain
     )
     grad_normed_out = jnp.dot(upstream, output_w, preferred_element_type=jnp.float32)
     scaled_grad = grad_normed_out * mixer_gain
@@ -312,8 +468,11 @@
     grad_gated = (
         inv_norm * scaled_grad - gated * (inv_norm * inv_norm * inv_norm) * (cross / INNER)[:, None]
     )
+    grad_scanned, grad_values, grad_gate_in, grad_skip_gain = after_pull(grad_gated)
+    scan_values, grad_maps, grad_step, grad_cum = scan_backward(
+        low_values, low_maps, step_sizes, cum, kept, grad_scanned
+    )
     (
-        grad_gate_in,
         grad_values_in,
         grad_state_part,
         grad_step_in,
@@ -323,8 +482,7 @@
         grad_shift_part,
         grad_step_bias,
         grad_decay_log,
-        grad_skip_gain,
-    ) = core_pull(grad_gated)
+    ) = before_pull((grad_values + scan_values, grad_maps, grad_step, grad_cum))
     (own_state,) = exchange(2, ("scatter", "tensor", grad_state_part.astype(jnp.bfloat16)))
     own_state = own_state.astype(jnp.bfloat16)
     low_gate = grad_gate_in.astype(jnp.bfloat16)

time: 545 us -> 313 us (0.57); the launches traced: 536 us -> 312 us
  matrix products: 154 us -> 30 us
  other arithmetic: 115 us -> 35 us
  local copies, waits for them, and re-layouts: 105 us -> 26.8 us
  Pallas kernels: 145 us -> 202 us
    dot_general x56 -> x2, matrix products: 123 us -> 0.76 us  [before_scan(): cum = jnp.einsum('ij,bjh->bih', lower, changes, precision=HIGHEST)]
    another operation x42 -> x2, other arithmetic: 48.9 us -> 1.45 us
    pallas_call x0 -> x2, Pallas kernels: none -> 41.9 us  [the longest x1 29.3 us: scan_backward(): pl.pallas_call(backward_kernel, grid=(blocks,), out_shape=(jax.ShapeDtype...]
    reshape x10 -> x2, local copies, waits for them, and re-layouts: 31.4 us -> 0.28 us  [the longest x1 0.2 us: before_scan(): return (values, maps, step_sizes, cum.reshape(length, heads))]
    squeeze x16 -> x0, local copies, waits for them, and re-layouts: 24.4 us -> none  [mixer_core(): lax.scan(jax.checkpoint(partial(block_scan, decay_rate=decay_rate)), init...]
    dynamic_update_slice x12 -> x0, other arithmetic: 16 us -> none  [mixer_core(): lax.scan(jax.checkpoint(partial(block_scan, decay_rate=decay_rate)), init...]
    another operation x29 -> x1, local copies, waits for them, and re-layouts: 16.6 us -> 0.85 us
    pallas_call x6, Pallas kernels: 145 us -> 160 us  [exchange(): pl.pallas_call(partial(exchange_kernel, tuple(plan), sizes), out_shape=tu...]
  transfers between devices with their start and end apart: 3 -> 3, of which waited for: 0 -> 1; matrix products, arithmetic and copies ran while one was open for 63% -> 21% of each run, Pallas kernels for 26% -> 62%
where the time goes in v2:
time: 313 us; the launch traced here: 312 us
  Pallas kernels  202 us (65%)
  other arithmetic  35 us (11%)
  matrix products  30 us (10%)
  local copies, waits for them, and re-layouts  26.8 us (9%)
  between operations  15.2 us (5%)
  waiting for transfers between devices  3.69 us (1%)
    pallas_call x6, Pallas kernels, exchange(): pl.pallas_call(partial(exchange_kernel, tuple(plan), sizes), out_shape=tu...  160 us
    pallas_call x1, Pallas kernels, scan_backward(): pl.pallas_call(backward_kernel, grid=(blocks,), out_shape=(jax.ShapeDtype...  29.3 us
    unnamed x124, local copies, waits for them, and re-layouts  16.9 us
    pallas_call x1, Pallas kernels, scan_forward(): pl.pallas_call(forward_kernel, grid=(blocks,), out_shape=(jax.ShapeDtypeS...  12.6 us
    dot_general x5, matrix products, times_transposed(): lax.dot_general(left_side, right_side, (((1,), (1,)), ((), ())), preferre...  9.27 us
    dot_general x4, matrix products, project(): return jnp.dot(normed, weight, preferred_element_type=jnp.float32)  8.31 us
    reduce_sum x2, other arithmetic, causal_conv(): summed = summed + kernel[offset] * padded[offset:offset + length]  7.43 us
    dot_general x1, matrix products, on_device(): jnp.dot(upstream, output_w, preferred_element_type=jnp.float32)  6.89 us
  transfers between devices with their start and end apart: 3, of which 1 were waited for; matrix products, arithmetic and copies ran while one was open for 21% of the time, Pallas kernels for 62%

profile of v2, /device:TPU:9, one launch (start us, length us, event | category | flops | bytes accessed | tf_op | source)
XLA Modules:
  0.0 312.4 jit_solution(5581651521932779963)
XLA Ops:
  8.8 1.2 fusion.12
  10.6 0.8 copy.55
  11.5 1.2 fusion.14.refs_0_
  13.6 50.5 %shard_map.288 = (bf16[1024,1024]{1,0:T(8,128)(2,1)S(1)}, bf16[1024,512]{1,0:T(8,128)(2,1)S(1)}, bf16[1024,512]{1,0:T(8,128)(2,1)S(1)}, bf16[1024,384]{1,0:T(8,128)(2,1)S(1)}) custom-call(bf16[256,1024]{1,0:T(8,128)(2,1)S(1)} %fusion.14.refs_0_, bf16[128,512]{1,0:T(8,128)(2,1)S(1)} %copy-done.26, bf16[128,512]{1,0:T(8,128)(2,1)S(1)} %copy-done.27, ...), custom_call_target="tpu_custom_call" | custom-call | tf_op jit(solution)/shard_map/pallas_call | solution.py:359
  64.1 1.0 copy-done.28
  65.2 2.0 broadcast_multiply_fusion.8
  68.0 2.5 fusion.32
  70.5 1.8 fusion.9
  72.9 1.2 fusion.59
  74.2 2.8 fusion.48
  77.0 12.6 %shard_map.289 = (f32[1024,512]{1,0:T(8,128)S(1)}, f32[4,512,128]{2,1,0:T(8,128)S(1)}) custom-call(bf16[1024,512]{1,0:T(8,128)(2,1)S(1)} %get-tuple-element.129.values_ref, bf16[1024,256]{1,0:T(8,128)(2,1)S(1)} %get-tuple-element.127.maps_ref, f32[1024,8]{1,0:T(8,128)S(1)} %get-tuple-element.126.step_ref, f32[1024,8]{1,0:T(8,128)S(1)} %copy.58.cum_ref, ...), custom_call_target="tpu_custom_call" | custom-call | tf_op jit(solution)/shard_map/pallas_call | solution.py:171
  89.7 1.3 copy-done.14
  91.0 1.0 copy-done.18
  91.9 2.6 fusion.60
  94.5 2.3 all-gather.3.cloned.1.call-done
  96.8 6.9 %multiply_reduce_fusion.7 = (f32[1024]{0:T(1024)S(1)}, f32[1024]{0:T(1024)S(1)}, f32[1024,512]{1,0:T(8,128)S(1)}, f32[1024,512]{1,0:T(8,128)}) fusion(f32[512]{0:T(512)S(1)} %copy-done.42, f32[1024,512]{1,0:T(8,128)} %fusion.60, f32[1024]{0:T(1024)S(1)} %fusion.46, f32[1024,512]{1,0:T(8,128)S(1)} %copy-done.15, f32[1024,512]{1,0:T(8,128)} %get-tuple-element.130, ...), kind=kOutput, calls=%fused_computation.29 | convolution fusion | flops 1084749824 | bytes 13647872 | tf_op jit(solution)/shard_map/dot_general | solution.py:453
  103.7 6.4 %shard_map.290 = f32[8,1024]{1,0:T(8,128)S(1)} custom-call(f32[8,1024]{1,0:T(8,128)S(1)} %select_maximum_fusion.2.refs_0_), custom_call_target="tpu_custom_call" | custom-call | tf_op jit(solution)/shard_map/pallas_call | solution.py:359
  110.2 3.2 %fusion.47 = f32[1024,1024]{1,0:T(8,128)} fusion(bf16[1024,512]{1,0:T(8,128)(2,1)S(1)} %copy-done.40, f32[1024,512]{1,0:T(8,128)S(1)} %get-tuple-element.124, f32[1024]{0:T(1024)S(1)} %bitcast.99, f32[512]{0:T(512)S(1)} %copy-done.42), kind=kOutput, calls=%fused_computation.132 | convolution fusion | flops 1075314688 | bytes 7346176 | tf_op jit(solution)/shard_map/dot_general | solution.py:382
  113.6 6.8 %multiply_reduce_fusion = (f32[512]{0:T(512)}, f32[1024,512]{1,0:T(8,128)S(1)}, bf16[1024,512]{1,0:T(8,128)(2,1)}, f32[512]{0:T(512)}) fusion(f32[1024,512]{1,0:T(8,128)} %get-tuple-element.130, f32[1024]{0:T(1024)S(1)} %fusion.46, f32[1024,512]{1,0:T(8,128)} %fusion.60, f32[1024]{0:T(1024)S(1)} %bitcast.114, f32[1024,512]{1,0:T(8,128)} %copy-done.32, ...), kind=kLoop, calls=%fused_computation.19 | loop fusion | flops 18349056 | bytes 13656064 | tf_op jit(solution)/shard_map/transpose(jvp())/reduce_sum | solution.py:243
  120.4 29.3 %shard_map.291 = (f32[1024,512]{1,0:T(8,128)S(1)}, f32[1024,256]{1,0:T(8,128)S(1)}, f32[1024,8]{1,0:T(8,128)S(1)}, f32[1024,8]{1,0:T(8,128)S(1)}, f32[8,1024]{1,0:T(8,128)S(1)}) custom-call(bf16[1024,512]{1,0:T(8,128)(2,1)S(1)} %get-tuple-element.129.values_ref, bf16[1024,256]{1,0:T(8,128)(2,1)S(1)} %copy-done.5, f32[1024,8]{1,0:T(8,128)S(1)} %copy-done.3, ...), custom_call_target="tpu_custom_call" | custom-call | tf_op jit(solution)/shard_map/pallas_call | solution.py:197
  149.7 1.3 copy-done.12
  151.0 1.0 copy-done.20
  152.0 0.8 copy-done.24
  152.8 0.8 copy-done.25
  153.6 1.2 copy.60
  155.0 1.0 copy.61
  156.0 2.8 fusion.49
  159.2 0.9 copy.64
  160.1 4.7 %multiply_reduce_fusion.11 = (f32[256]{0:T(256)}, f32[256]{0:T(256)}, f32[256]{0:T(256)}, f32[256]{0:T(256)}, f32[256]{0:T(256)}, /*index=5*/f32[1024,256]{1,0:T(8,128)S(1)}) fusion(f32[1024,256]{1,0:T(8,128)} %copy-done.37, f32[1024,256]{1,0:T(8,128)} %get-tuple-element.128, f32[1024,256]{1,0:T(8,128)S(1)} %copy-done.21), kind=kLoop, calls=%fused_computation.72 | loop fusion | flops 4717312 | bytes 4199424 | tf_op jit(solution)/shard_map/transpose(jvp())/reduce_sum | solution.py:28
  165.4 28.8 %shard_map.292 = f32[256,256]{1,0:T(8,128)S(1)} custom-call(bf16[1024,256]{1,0:T(8,128)(2,1)S(1)} %fusion.22.refs_0_), custom_call_target="tpu_custom_call" | custom-call | tf_op jit(solution)/shard_map/pallas_call | solution.py:359
  194.3 2.8 multiply_reduce_fusion.5
  197.0 1.3 broadcast_multiply_fusion
  198.3 1.1 fusion.5
  201.3 0.9 copy-done.11
  202.5 1.3 convolution_convert_fusion.2.refs_1_
  203.8 1.3 convolution_convert_fusion.1.refs_2_
  205.1 1.3 fusion.61
  207.3 1.4 fusion.8.refs_3_
  208.8 1.3 add_convert_fusion.refs_0_
  210.1 47.3 %shard_map.293 = (f32[256,1024]{1,0:T(8,128)S(1)}, f32[128,512]{1,0:T(8,128)S(1)}, f32[128,512]{1,0:T(8,128)S(1)}, f32[128,512]{1,0:T(8,128)S(1)}, f32[128,384]{1,0:T(8,128)S(1)}) custom-call(bf16[1024,1024]{1,0:T(8,128)(2,1)S(1)} %add_convert_fusion.refs_0_, bf16[1024,512]{1,0:T(8,128)(2,1)S(1)} %convolution_convert_fusion.2.refs_1_, ...), custom_call_target="tpu_custom_call" | custom-call | tf_op jit(solution)/shard_map/pallas_call | solution.py:359
  259.4 0.7 add_bitcast_fusion
  261.4 1.2 negate_multiply_fusion
  262.6 0.8 concatenate.16
  264.8 2.8 fusion.21
  267.5 1.5 copy.65
  269.0 19.2 %shard_map.294 = (f32[8,1024]{1,0:T(8,128)S(1)}, f32[128,256]{1,0:T(8,128)S(1)}) custom-call(f32[8,1024]{1,0:T(8,128)S(1)} %reshape.198.refs_0_, f32[128,256]{1,0:T(8,128)S(1)} %slice.122.refs_1_), custom_call_target="tpu_custom_call" | custom-call | tf_op jit(solution)/shard_map/pallas_call | solution.py:359
  288.3 7.4 %shard_map.295 = (f32[8,1024]{1,0:T(8,128)S(1)}, f32[8,512]{1,0:T(8,128)S(1)}) custom-call(f32[8,1024]{1,0:T(8,128)S(1)} %get-tuple-element.49.refs_0_, f32[8,512]{1,0:T(8,128)S(1)} %reshape.205.refs_1_), custom_call_target="tpu_custom_call" | custom-call | tf_op jit(solution)/shard_map/pallas_call | solution.py:359
  300.0 3.1 fusion.18
  (161 shorter events, 19.9 us)
Async XLA Ops:
  7.2 5.5 %copy-start.41 = (bf16[128,256]{1,0:T(8,128)(2,1)S(1)}, bf16[128,256]{1,0:T(8,128)(2,1)}, u32[]{:S(2)}) copy-start(bf16[128,256]{1,0:T(8,128)(2,1)} %param.22) | copy-start | bytes 196612
  7.2 5.6 %copy-start.56 = (f32[8]{0:T(128)S(1)}, f32[8]{0:T(128)}, u32[]{:S(2)}) copy-start(f32[8]{0:T(128)} %param.29) | copy-start | bytes 100
  7.2 6.3 %copy-start.53 = (f32[8]{0:T(128)S(1)}, f32[8]{0:T(128)}, u32[]{:S(2)}) copy-start(f32[8]{0:T(128)} %param.30) | copy-start | bytes 100
  7.2 6.4 %copy-start.27 = (bf16[128,512]{1,0:T(8,128)(2,1)S(1)}, bf16[128,512]{1,0:T(8,128)(2,1)}, u32[]{:S(2)}) copy-start(bf16[128,512]{1,0:T(8,128)(2,1)} %refs_2_.1) | copy-start | bytes 393220
  7.2 6.4 %copy-start.26 = (bf16[128,512]{1,0:T(8,128)(2,1)S(1)}, bf16[128,512]{1,0:T(8,128)(2,1)}, u32[]{:S(2)}) copy-start(bf16[128,512]{1,0:T(8,128)(2,1)} %refs_1_.1) | copy-start | bytes 393220
  7.2 57.9 %copy-start.55 = (f32[8]{0:T(128)S(1)}, f32[8]{0:T(128)}, u32[]{:S(2)}) copy-start(f32[8]{0:T(128)} %param.28) | copy-start | bytes 100
  7.2 87.3 %all-gather.5.cloned.1.call-start = ((), (), s32[]{:S(2)}) async-start(), calls=%async_computation.2 | async-start | bytes 1179648 | tf_op jit(solution)/shard_map/all_gather | solution.py:429
  8.0 88.9 %all-gather.3.cloned.1.call-start = ((), (), s32[]{:S(2)}) async-start(), calls=%async_computation.1 | async-start | bytes 2621440 | tf_op jit(solution)/shard_map/all_gather | solution.py:430
  8.7 291.3 %reduce-scatter.2.cloned.1.call-start = ((), (), s32[]{:S(2)}) async-start(), calls=%async_computation.3 | async-start | bytes 5242880 | tf_op jit(solution)/shard_map/reduce_scatter | solution.py:462
  10.6 54.5 %copy-start.43 = (f32[256]{0:T(256)}, f32[256]{0:T(256)S(1)}, u32[]{:S(2)}) copy-start(f32[256]{0:T(256)S(1)} %get-tuple-element.162) | copy-start | bytes 3076
  12.7 54.5 %copy-start = (bf16[256,1024]{1,0:T(8,128)(2,1)}, bf16[256,1024]{1,0:T(8,128)(2,1)S(1)}, u32[]{:S(2)}) copy-start(bf16[256,1024]{1,0:T(8,128)(2,1)S(1)} %fusion.14.refs_0_) | copy-start | bytes 1572868
  65.1 2.6 copy-start.8
  65.1 2.9 copy-start.22
  65.1 7.2 %copy-start.16 = (bf16[1024,512]{1,0:T(8,128)(2,1)}, bf16[1024,512]{1,0:T(8,128)(2,1)S(1)}, u32[]{:S(2)}) copy-start(bf16[1024,512]{1,0:T(8,128)(2,1)S(1)} %get-tuple-element.37) | copy-start | bytes 3145732
  65.1 2.8 copy-start.47
  65.2 2.8 copy-start.46
  67.2 9.8 %copy-start.2 = (f32[1024,8]{1,0:T(8,128)}, f32[1024,8]{1,0:T(8,128)S(1)}, u32[]{:S(2)}) copy-start(f32[1024,8]{1,0:T(8,128)S(1)} %get-tuple-element.126.step_ref) | copy-start | bytes 98308
  68.0 9.0 %copy-start.6 = (f32[1024,8]{1,0:T(8,128)}, f32[1024,8]{1,0:T(8,128)S(1)}, u32[]{:S(2)}) copy-start(f32[1024,8]{1,0:T(8,128)S(1)} %copy.58.cum_ref) | copy-start | bytes 98308
  68.0 2.5 copy-start.52
  70.5 3.6 %copy-start.37 = (f32[1024,256]{1,0:T(8,128)}, f32[1024,256]{1,0:T(8,128)S(1)}, u32[]{:S(2)}) copy-start(f32[1024,256]{1,0:T(8,128)S(1)} %fusion.32) | copy-start | bytes 3145732
  70.5 2.4 copy-start.9
  72.3 4.6 %copy-start.4 = (bf16[1024,256]{1,0:T(8,128)(2,1)}, bf16[1024,256]{1,0:T(8,128)(2,1)S(1)}, u32[]{:S(2)}) copy-start(bf16[1024,256]{1,0:T(8,128)(2,1)S(1)} %get-tuple-element.127.maps_ref) | copy-start | bytes 1572868
  74.1 2.8 copy-start.35
  77.0 15.0 %copy-start.29 = (bf16[1024,512]{1,0:T(8,128)(2,1)S(1)}, bf16[1024,512]{1,0:T(8,128)(2,1)}, u32[]{:S(2)}) copy-start(bf16[1024,512]{1,0:T(8,128)(2,1)} %copy-done.28) | copy-start | bytes 3145732
  91.9 4.9 %copy-start.15 = (f32[1024,512]{1,0:T(8,128)S(1)}, f32[1024,512]{1,0:T(8,128)}, u32[]{:S(2)}) copy-start(f32[1024,512]{1,0:T(8,128)} %copy-done.14) | copy-start | bytes 6291460
  91.9 4.9 %copy-start.42 = (f32[512]{0:T(512)S(1)}, f32[512]{0:T(512)}, u32[]{:S(2)}) copy-start(f32[512]{0:T(512)} %param.31) | copy-start | bytes 6148
  96.8 13.4 %copy-start.40 = (bf16[1024,512]{1,0:T(8,128)(2,1)S(1)}, bf16[1024,512]{1,0:T(8,128)(2,1)}, u32[]{:S(2)}) copy-start(bf16[1024,512]{1,0:T(8,128)(2,1)} %all-gather.5.cloned.1.call-done) | copy-start | bytes 3145732
  103.7 6.5 %copy-start.32 = (f32[1024,512]{1,0:T(8,128)}, f32[1024,512]{1,0:T(8,128)S(1)}, u32[]{:S(2)}) copy-start(f32[1024,512]{1,0:T(8,128)S(1)} %get-tuple-element.124) | copy-start | bytes 6291460
  113.5 6.9 %copy-start.3 = (f32[1024,8]{1,0:T(8,128)S(1)}, f32[1024,8]{1,0:T(8,128)}, u32[]{:S(2)}) copy-start(f32[1024,8]{1,0:T(8,128)} %copy-done.2) | copy-start | bytes 98308
  113.5 6.9 %copy-start.5 = (bf16[1024,256]{1,0:T(8,128)(2,1)S(1)}, bf16[1024,256]{1,0:T(8,128)(2,1)}, u32[]{:S(2)}) copy-start(bf16[1024,256]{1,0:T(8,128)(2,1)} %copy-done.4) | copy-start | bytes 1572868
  113.5 6.9 %copy-start.7 = (f32[1024,8]{1,0:T(8,128)S(1)}, f32[1024,8]{1,0:T(8,128)}, u32[]{:S(2)}) copy-start(f32[1024,8]{1,0:T(8,128)} %copy-done.6) | copy-start | bytes 98308
  113.5 6.8 %copy-start.19 = (f32[4,512,128]{2,1,0:T(8,128)S(1)}, f32[4,512,128]{2,1,0:T(8,128)}, u32[]{:S(2)}) copy-start(f32[4,512,128]{2,1,0:T(8,128)} %copy-done.18) | copy-start | bytes 3145732
  156.0 2.8 copy-start.10
  156.0 4.0 %copy-start.21 = (f32[1024,256]{1,0:T(8,128)S(1)}, f32[1024,256]{1,0:T(8,128)}, u32[]{:S(2)}) copy-start(f32[1024,256]{1,0:T(8,128)} %copy-done.20) | copy-start | bytes 3145732
  164.7 29.5 %copy-start.36 = (f32[1024,512]{1,0:T(8,128)S(1)}, f32[1024,512]{1,0:T(8,128)}, u32[]{:S(2)}) copy-start(f32[1024,512]{1,0:T(8,128)} %copy-done.35) | copy-start | bytes 6291460
  165.1 29.2 %copy-start.13 = (f32[1024,512]{1,0:T(8,128)S(1)}, f32[1024,512]{1,0:T(8,128)}, u32[]{:S(2)}) copy-start(f32[1024,512]{1,0:T(8,128)} %copy-done.12) | copy-start | bytes 6291460
  165.1 29.2 %copy-start.31 = (f32[1024,512]{1,0:T(8,128)S(1)}, f32[1024,512]{1,0:T(8,128)}, u32[]{:S(2)}) copy-start(f32[1024,512]{1,0:T(8,128)} %get-tuple-element.130) | copy-start | bytes 6291460
  198.3 1.5 copy-start.39
  200.6 1.6 copy-start.11
  200.6 1.9 copy-start.38
  205.1 1.6 copy-start.33
  205.1 2.2 copy-start.54
  210.1 48.0 %copy-start.45 = (f32[512]{0:T(512)S(1)}, f32[512]{0:T(512)}, u32[]{:S(2)}) copy-start(f32[512]{0:T(512)} %get-tuple-element.118) | copy-start | bytes 6148
  210.1 48.1 %copy-start.48 = (f32[256]{0:T(256)S(1)}, f32[256]{0:T(256)}, u32[]{:S(2)}) copy-start(f32[256]{0:T(256)} %get-tuple-element.109) | copy-start | bytes 3076
  210.1 48.1 %copy-start.49 = (f32[256]{0:T(256)S(1)}, f32[256]{0:T(256)}, u32[]{:S(2)}) copy-start(f32[256]{0:T(256)} %get-tuple-element.110) | copy-start | bytes 3076
  210.1 54.7 %copy-start.34 = (bf16[256,1024]{1,0:T(8,128)(2,1)S(1)}, bf16[256,1024]{1,0:T(8,128)(2,1)}, u32[]{:S(2)}) copy-start(bf16[256,1024]{1,0:T(8,128)(2,1)} %param.17) | copy-start | bytes 1572868
  264.8 2.8 copy-start.44
  264.8 2.8 copy-start.50
  (12 other events, 13.5 us)
Sparse Core Ops, SparseCore 0:
  10.0 41.5 all-gather.4
  53.1 43.6 all-gather.2
  113.6 89.2 reduce-scatter.1

commit v3 on v2

--- a/solution.py
+++ b/solution.py
@@ -417,16 +417,16 @@
     small_w = jnp.concatenate(
         [proj_state, proj_step, jnp.zeros((proj_step.shape[0], tail), jnp.bfloat16)], axis=1
     )
-    normed, gate_w, values_w, small_w = exchange(
+    normed, gate_w, values_w, output_w, small_w = exchange(
         0,
         ("gather", "tensor", normed_rows),
         ("gather", "dp", proj_gate),
         ("gather", "dp", proj_values),
+        ("gather", "dp", proj_output),
         ("gather", "dp", small_w),
     )
     state_w = small_w[:, :state_columns]
     step_w = small_w[:, state_columns : state_columns + head_count]
-    output_w = lax.all_gather(proj_output, "dp", axis=0, tiled=True)
     upstream = lax.all_gather(out_grad, "tensor", axis=0, tiled=True)
     gate_in = project(normed, gate_w)
     values_in = project(normed, values_w)
@@ -460,9 +460,12 @@
     cross = row_sums[1]
     normed_out = (gated * inv_norm * mixer_gain).astype(jnp.bfloat16)
     mixed_rows = lax.psum_scatter(
-        times_transposed(normed_out, output_w), "tensor", scatter_dimension=0, tiled=True
-    )
-    layer_output = (rows_in + mixed_rows).astype(jnp.bfloat16)
+        times_transposed(normed_out, output_w).astype(jnp.bfloat16),
+        "tensor",
+        scatter_dimension=0,
+        tiled=True,
+    )
+    layer_output = (rows_in + mixed_rows.astype(jnp.float32)).astype(jnp.bfloat16)
     grad_output_w = contract_rows(upstream, normed_out)
     grad_mixer_gain = jnp.sum(grad_normed_out * gated * inv_norm, axis=0)
     grad_gated = (
@@ -483,7 +486,11 @@
         grad_step_bias,
         grad_decay_log,
     ) = before_pull((grad_values + scan_values, grad_maps, grad_step, grad_cum))
-    (own_state,) = exchange(2, ("scatter", "tensor", grad_state_part.astype(jnp.bfloat16)))
+    own_state, owned_output = exchange(
+        2,
+        ("scatter", "tensor", grad_state_part.astype(jnp.bfloat16)),
+        ("scatter", "dp", grad_output_w.astype(jnp.bfloat16)),
+    )
     own_state = own_state.astype(jnp.bfloat16)
     low_gate = grad_gate_in.astype(jnp.bfloat16)
     low_values = grad_values_in.astype(jnp.bfloat16)
@@ -501,12 +508,11 @@
     summed = times_transposed(low_gate, gate_w)
     summed = summed + times_transposed(low_values, values_w)
     head_part = summed + times_transposed(low_step, step_w)
-    head_part, owned_gate, owned_values, owned_output, owned_small = exchange(
+    head_part, owned_gate, owned_values, owned_small = exchange(
         3,
         ("scatter", "tensor", head_part.astype(jnp.bfloat16)),
         ("scatter", "dp", grad_gate_w.astype(jnp.bfloat16)),
         ("scatter", "dp", grad_values_w.astype(jnp.bfloat16)),
-        ("scatter", "dp", grad_output_w.astype(jnp.bfloat16)),
         ("scatter", "dp", grad_small_w.astype(jnp.bfloat16)),
     )
     grad_normed_rows = head_part + times_transposed(own_state, state_w)
@@ -537,7 +543,7 @@
     shared_sum, owned_state = exchange(
         4,
         ("sum", "tensor", packed(shared, width)),
-        ("sum", "tensor", owned_small[:, :state_columns]),
+        ("sum", "tensor", owned_small[:, :state_columns].astype(jnp.bfloat16)),
     )
     own = [
         grad_conv_values,

time: 313 us -> 313 us (level)
  Pallas kernels: 202 us -> 217 us
  local copies, waits for them, and re-layouts: 26.8 us -> 20 us
  other arithmetic: 35 us -> 28.6 us
    pallas_call x6, Pallas kernels: 160 us -> 176 us  [exchange(): pl.pallas_call(partial(exchange_kernel, tuple(plan), sizes), out_shape=tu...]
    unnamed x124 -> x96, local copies, waits for them, and re-layouts: 16.9 us -> 12.6 us
  transfers between devices with their start and end apart: 3 -> 2, of which waited for: 1 -> 0; matrix products, arithmetic and copies ran while one was open for 21% -> 18% of each run, Pallas kernels for 62% -> 68%
where the time goes in v3:
time: 313 us
  Pallas kernels  217 us (69%)
  matrix products  30.7 us (10%)
  other arithmetic  28.6 us (9%)
  local copies, waits for them, and re-layouts  20 us (6%)
  between operations  15.4 us (5%)
    pallas_call x6, Pallas kernels, exchange(): pl.pallas_call(partial(exchange_kernel, tuple(plan), sizes), out_shape=tu...  176 us
    pallas_call x1, Pallas kernels, scan_backward(): pl.pallas_call(backward_kernel, grid=(blocks,), out_shape=(jax.ShapeDtype...  29.1 us
    unnamed x96, local copies, waits for them, and re-layouts  12.6 us
    pallas_call x1, Pallas kernels, scan_forward(): pl.pallas_call(forward_kernel, grid=(blocks,), out_shape=(jax.ShapeDtypeS...  12.4 us
    dot_general x5, matrix products, times_transposed(): lax.dot_general(left_side, right_side, (((1,), (1,)), ((), ())), preferre...  9.42 us
    dot_general x4, matrix products, project(): return jnp.dot(normed, weight, preferred_element_type=jnp.float32)  8.23 us
    dot_general x1, matrix products, on_device(): jnp.dot(upstream, output_w, preferred_element_type=jnp.float32)  7.52 us
    reduce_sum x2, other arithmetic, causal_conv(): summed = summed + kernel[offset] * padded[offset:offset + length]  7 us
  transfers between devices with their start and end apart: 2, of which 0 were waited for; matrix products, arithmetic and copies ran while one was open for 18% of the time, Pallas kernels for 68%

profile of v3, /device:TPU:9, one launch (start us, length us, event | category | flops | bytes accessed | tf_op | source)
XLA Modules:
  0.0 312.7 jit_solution(9587669056219548364)
XLA Ops:
  7.3 0.7 all-gather.2.cloned.1.call-update
  8.0 1.2 fusion.14
  9.3 0.8 copy.57
  10.2 1.2 fusion.16.refs_0_
  12.3 84.4 %shard_map.288 = (bf16[1024,1024]{1,0:T(8,128)(2,1)S(1)}, bf16[1024,512]{1,0:T(8,128)(2,1)S(1)}, bf16[1024,512]{1,0:T(8,128)(2,1)S(1)}, bf16[1024,512]{1,0:T(8,128)(2,1)S(1)}, bf16[1024,384]{1,0:T(8,128)(2,1)S(1)}) custom-call(bf16[256,1024]{1,0:T(8,128)(2,1)S(1)} %fusion.16.refs_0_, bf16[128,512]{1,0:T(8,128)(2,1)S(1)} %copy-done.13, ...), custom_call_target="tpu_custom_call" | custom-call | tf_op jit(solution)/shard_map/pallas_call | solution.py:359
  96.7 1.0 copy-done.16
  97.6 1.0 copy-done.19
  98.7 2.0 broadcast_multiply_fusion.8
  101.5 2.4 fusion.34
  103.9 1.7 fusion.11
  106.3 1.3 fusion.60
  107.6 2.8 fusion.49
  110.4 12.4 %shard_map.289 = (f32[1024,512]{1,0:T(8,128)S(1)}, f32[4,512,128]{2,1,0:T(8,128)S(1)}) custom-call(bf16[1024,512]{1,0:T(8,128)(2,1)S(1)} %get-tuple-element.133.values_ref, bf16[1024,256]{1,0:T(8,128)(2,1)S(1)} %get-tuple-element.131.maps_ref, f32[1024,8]{1,0:T(8,128)S(1)} %get-tuple-element.130.step_ref, f32[1024,8]{1,0:T(8,128)S(1)} %copy.60.cum_ref, ...), custom_call_target="tpu_custom_call" | custom-call | tf_op jit(solution)/shard_map/pallas_call | solution.py:171
  122.8 1.3 copy-done.3
  124.1 1.0 copy-done.6
  125.1 2.5 fusion.61
  127.7 7.5 %multiply_reduce_fusion.6 = (f32[1024]{0:T(1024)S(1)}, f32[1024]{0:T(1024)S(1)}, f32[1024,512]{1,0:T(8,128)S(1)}, f32[512,1024]{0,1:T(8,128)}) fusion(f32[512]{0:T(512)S(1)} %copy-done.37, f32[1024,512]{1,0:T(8,128)} %fusion.61, f32[1024]{0:T(1024)S(1)} %fusion.48, f32[1024,512]{1,0:T(8,128)} %copy-done.3, f32[1024,512]{1,0:T(8,128)} %get-tuple-element.134, ...), kind=kOutput, calls=%fused_computation.32 | convolution fusion | flops 1084749824 | bytes 13647872 | tf_op jit(solution)/shard_map/dot_general | solution.py:453
  135.2 4.2 %shard_map.290 = f32[8,1024]{1,0:T(8,128)S(1)} custom-call(f32[8,1024]{1,0:T(8,128)S(1)} %select_maximum_fusion.2.refs_0_), custom_call_target="tpu_custom_call" | custom-call | tf_op jit(solution)/shard_map/pallas_call | solution.py:359
  139.4 2.6 convolution_convert_fusion
  142.1 6.2 %multiply_reduce_fusion = (f32[512]{0:T(512)S(1)}, f32[1024,512]{1,0:T(8,128)S(1)}, bf16[1024,512]{1,0:T(8,128)(2,1)}, f32[512]{0:T(512)S(1)}) fusion(f32[1024,512]{1,0:T(8,128)} %get-tuple-element.134, f32[1024]{0:T(1024)S(1)} %fusion.48, f32[1024,512]{1,0:T(8,128)} %fusion.61, f32[1024]{0:T(1024)S(1)} %bitcast.130, f32[1024,512]{1,0:T(8,128)} %copy-done.28, ...), kind=kLoop, calls=%fused_computation.23 | loop fusion | flops 18349056 | bytes 13656064 | tf_op jit(solution)/shard_map/transpose(jvp())/reduce_sum | solution.py:243
  148.3 29.1 %shard_map.291 = (f32[1024,512]{1,0:T(8,128)S(1)}, f32[1024,256]{1,0:T(8,128)S(1)}, f32[1024,8]{1,0:T(8,128)S(1)}, f32[1024,8]{1,0:T(8,128)S(1)}, f32[8,1024]{1,0:T(8,128)S(1)}) custom-call(bf16[1024,512]{1,0:T(8,128)(2,1)S(1)} %get-tuple-element.133.values_ref, bf16[1024,256]{1,0:T(8,128)(2,1)S(1)} %get-tuple-element.131.maps_ref, ...), custom_call_target="tpu_custom_call" | custom-call | tf_op jit(solution)/shard_map/pallas_call | solution.py:197
  177.4 0.8 copy-done.11
  178.2 2.9 multiply_reduce_fusion.4
  181.1 1.3 copy.63
  182.7 1.0 copy.64
  183.7 1.9 fusion.50
  185.6 0.7 copy-done.26
  186.7 0.9 copy.67
  187.6 4.1 %multiply_reduce_fusion.10 = (f32[256]{0:T(256)S(1)}, f32[256]{0:T(256)S(1)}, f32[256]{0:T(256)S(1)}, f32[256]{0:T(256)S(1)}, f32[256]{0:T(256)S(1)}, /*index=5*/f32[1024,256]{1,0:T(8,128)S(1)}) fusion(f32[1024,256]{1,0:T(8,128)} %copy-done.25, f32[1024,256]{1,0:T(8,128)} %get-tuple-element.132, f32[1024,256]{1,0:T(8,128)} %copy-done.8), kind=kLoop, calls=%fused_computation.76 | loop fusion | flops 4717312 | bytes 4199424 | tf_op jit(solution)/shard_map/transpose(jvp())/reduce_sum | solution.py:28
  192.4 1.2 copy-done.29
  194.2 1.4 fusion.10.refs_1_
  195.6 17.4 %shard_map.292 = (f32[256,256]{1,0:T(8,128)S(1)}, f32[128,512]{1,0:T(8,128)S(1)}) custom-call(bf16[1024,256]{1,0:T(8,128)(2,1)S(1)} %fusion.24.refs_0_, bf16[1024,512]{1,0:T(8,128)(2,1)S(1)} %fusion.10.refs_1_), custom_call_target="tpu_custom_call" | custom-call | tf_op jit(solution)/shard_map/pallas_call | solution.py:359
  213.4 1.3 broadcast_multiply_fusion
  214.7 1.1 fusion.5
  216.0 1.7 fusion.41
  217.8 1.3 convolution_convert_fusion.3.refs_1_
  219.1 1.3 convolution_convert_fusion.2.refs_2_
  220.4 1.3 fusion.62
  221.7 1.3 add_convert_fusion.refs_0_
  223.0 49.5 %shard_map.293 = (f32[256,1024]{1,0:T(8,128)S(1)}, f32[128,512]{1,0:T(8,128)S(1)}, f32[128,512]{1,0:T(8,128)S(1)}, f32[128,384]{1,0:T(8,128)S(1)}) custom-call(bf16[1024,1024]{1,0:T(8,128)(2,1)S(1)} %add_convert_fusion.refs_0_, bf16[1024,512]{1,0:T(8,128)(2,1)S(1)} %convolution_convert_fusion.3.refs_1_, ...), custom_call_target="tpu_custom_call" | custom-call | tf_op jit(solution)/shard_map/pallas_call | solution.py:359
  273.0 2.5 fusion.23
  275.5 0.7 copy.68
  276.2 10.9 %shard_map.294 = (f32[8,1024]{1,0:T(8,128)S(1)}, f32[128,256]{1,0:T(8,128)S(1)}) custom-call(f32[8,1024]{1,0:T(8,128)S(1)} %reshape.198.refs_0_, bf16[128,256]{1,0:T(8,128)(2,1)S(1)} %slice.178.refs_1_), custom_call_target="tpu_custom_call" | custom-call | tf_op jit(solution)/shard_map/pallas_call | solution.py:359
  287.1 9.4 %shard_map.295 = (f32[8,1024]{1,0:T(8,128)S(1)}, f32[8,512]{1,0:T(8,128)S(1)}) custom-call(f32[8,1024]{1,0:T(8,128)S(1)} %get-tuple-element.53.refs_0_, f32[8,512]{1,0:T(8,128)S(1)} %reshape.205.refs_1_), custom_call_target="tpu_custom_call" | custom-call | tf_op jit(solution)/shard_map/pallas_call | solution.py:359
  300.1 3.1 fusion.20
  303.1 0.7 copy.85
  303.8 0.7 copy.86
  305.2 0.7 copy.88
  (130 shorter events, 9.0 us)
Async XLA Ops:
  7.2 4.2 %copy-start.32 = (bf16[128,256]{1,0:T(8,128)(2,1)S(1)}, bf16[128,256]{1,0:T(8,128)(2,1)}, u32[]{:S(2)}) copy-start(bf16[128,256]{1,0:T(8,128)(2,1)} %param.22) | copy-start | bytes 196612
  7.2 4.2 %copy-start.42 = (f32[8]{0:T(128)S(1)}, f32[8]{0:T(128)}, u32[]{:S(2)}) copy-start(f32[8]{0:T(128)} %param.29) | copy-start | bytes 100
  7.2 4.9 %copy-start.39 = (f32[8]{0:T(128)S(1)}, f32[8]{0:T(128)}, u32[]{:S(2)}) copy-start(f32[8]{0:T(128)} %param.30) | copy-start | bytes 100
  7.2 5.1 %copy-start.15 = (bf16[128,512]{1,0:T(8,128)(2,1)S(1)}, bf16[128,512]{1,0:T(8,128)(2,1)}, u32[]{:S(2)}) copy-start(bf16[128,512]{1,0:T(8,128)(2,1)} %refs_3_.1) | copy-start | bytes 393220
  7.2 5.1 %copy-start.14 = (bf16[128,512]{1,0:T(8,128)(2,1)S(1)}, bf16[128,512]{1,0:T(8,128)(2,1)}, u32[]{:S(2)}) copy-start(bf16[128,512]{1,0:T(8,128)(2,1)} %refs_2_.1) | copy-start | bytes 393220
  7.2 5.0 %copy-start.13 = (bf16[128,512]{1,0:T(8,128)(2,1)S(1)}, bf16[128,512]{1,0:T(8,128)(2,1)}, u32[]{:S(2)}) copy-start(bf16[128,512]{1,0:T(8,128)(2,1)} %refs_1_.1) | copy-start | bytes 393220
  7.2 91.4 %copy-start.41 = (f32[8]{0:T(128)S(1)}, f32[8]{0:T(128)}, u32[]{:S(2)}) copy-start(f32[8]{0:T(128)} %param.28) | copy-start | bytes 100
  7.3 120.4 %all-gather.2.cloned.1.call-start = ((), (), s32[]{:S(2)}) async-start(), calls=%async_computation.1 | async-start | bytes 2621440 | tf_op jit(solution)/shard_map/all_gather | solution.py:430
  8.0 292.1 %reduce-scatter.2.cloned.1.call-start = ((), (), s32[]{:S(2)}) async-start(), calls=%async_computation.2 | async-start | bytes 2621440 | tf_op jit(solution)/shard_map/reduce_scatter | solution.py:462
  96.7 1.0 copy-start.16
  97.6 1.0 copy-start.19
  98.6 2.6 copy-start
  98.6 2.6 copy-start.9
  98.6 7.0 %copy-start.4 = (bf16[1024,512]{1,0:T(8,128)(2,1)}, bf16[1024,512]{1,0:T(8,128)(2,1)S(1)}, u32[]{:S(2)}) copy-start(bf16[1024,512]{1,0:T(8,128)(2,1)S(1)} %get-tuple-element.39) | copy-start | bytes 3145732
  98.6 2.8 copy-start.35
  98.6 2.8 copy-start.34
  101.5 2.4 copy-start.38
  103.9 3.6 %copy-start.25 = (f32[1024,256]{1,0:T(8,128)}, f32[1024,256]{1,0:T(8,128)S(1)}, u32[]{:S(2)}) copy-start(f32[1024,256]{1,0:T(8,128)S(1)} %fusion.34) | copy-start | bytes 3145732
  103.9 2.3 copy-start.1
  106.3 1.3 copy-start.36
  107.5 2.8 copy-start.22
  110.4 14.8 %copy-start.17 = (bf16[1024,512]{1,0:T(8,128)(2,1)S(1)}, bf16[1024,512]{1,0:T(8,128)(2,1)}, u32[]{:S(2)}) copy-start(bf16[1024,512]{1,0:T(8,128)(2,1)} %copy-done.16) | copy-start | bytes 3145732
  122.8 1.3 copy-start.3
  124.1 1.0 copy-start.6
  125.1 2.6 copy-start.37
  127.7 11.8 %copy-start.20 = (bf16[1024,512]{1,0:T(8,128)(2,1)S(1)}, bf16[1024,512]{1,0:T(8,128)(2,1)}, u32[]{:S(2)}) copy-start(bf16[1024,512]{1,0:T(8,128)(2,1)} %copy-done.19) | copy-start | bytes 3145732
  135.2 4.2 %copy-start.28 = (f32[1024,512]{1,0:T(8,128)}, f32[1024,512]{1,0:T(8,128)S(1)}, u32[]{:S(2)}) copy-start(f32[1024,512]{1,0:T(8,128)S(1)} %get-tuple-element.128) | copy-start | bytes 6291460
  142.1 6.2 %copy-start.7 = (f32[4,512,128]{2,1,0:T(8,128)S(1)}, f32[4,512,128]{2,1,0:T(8,128)}, u32[]{:S(2)}) copy-start(f32[4,512,128]{2,1,0:T(8,128)} %copy-done.6) | copy-start | bytes 3145732
  148.2 29.9 %copy-start.21 = (f32[1024,512]{1,0:T(8,128)S(1)}, f32[1024,512]{1,0:T(8,128)}, u32[]{:S(2)}) copy-start(f32[1024,512]{1,0:T(8,128)} %get-tuple-element.134) | copy-start | bytes 6291460
  148.2 29.9 %copy-start.23 = (f32[1024,512]{1,0:T(8,128)S(1)}, f32[1024,512]{1,0:T(8,128)}, u32[]{:S(2)}) copy-start(f32[1024,512]{1,0:T(8,128)} %copy-done.22) | copy-start | bytes 6291460
  177.4 0.8 copy-start.11
  178.2 2.9 copy-start.8
  178.2 2.9 copy-start.12
  181.1 5.2 %copy-start.2 = (bf16[1024,1024]{1,0:T(8,128)(2,1)S(1)}, bf16[1024,1024]{1,0:T(8,128)(2,1)}, u32[]{:S(2)}) copy-start(bf16[1024,1024]{1,0:T(8,128)(2,1)} %copy-done) | copy-start | bytes 6291460
  185.6 0.7 copy-start.26
  192.0 1.6 copy-start.29
  192.0 2.2 copy-start.40
  195.6 17.7 %copy-start.24 = (f32[1024,512]{1,0:T(8,128)S(1)}, f32[1024,512]{1,0:T(8,128)}, u32[]{:S(2)}) copy-start(f32[1024,512]{1,0:T(8,128)} %get-tuple-element.126) | copy-start | bytes 6291460
  214.7 1.1 copy-start.31
  214.7 1.3 copy-start.27
  216.0 1.8 copy-start.30
  219.1 1.3 copy-start.18
  220.4 1.3 copy-start.5
  223.0 50.0 %copy-start.10 = (bf16[1024,384]{1,0:T(8,128)(2,1)S(1)}, bf16[1024,384]{1,0:T(8,128)(2,1)}, u32[]{:S(2)}) copy-start(bf16[1024,384]{1,0:T(8,128)(2,1)} %copy-done.9) | copy-start | bytes 2359300
  223.0 50.0 %copy-start.33 = (f32[1024]{0:T(1024)S(1)}, f32[1024]{0:T(1024)}, u32[]{:S(2)}) copy-start(f32[1024]{0:T(1024)} %param.19) | copy-start | bytes 12292
Sparse Core Ops, SparseCore 0:
  9.7 83.2 all-gather.1
  142.2 43.5 reduce-scatter.1
